TPU v7x, 768 devices: a whole 4x8x12 slice. The times are simulated.
768 devices in a mesh: dp: 96 (over x, z, y_lo), tensor: 8 (over y_hi, core).
Axes of the slice: x: 4, y: 8 (y_hi: 4, y_lo: 2; y = y_hi * 2 + y_lo), z: 12, core: 2. Of those that a mesh axis runs over, the one named last changes fastest.
Arguments:
- activations: bfloat16 [36864, 8192], P('dp', 'tensor'), may hold values from -6 to 6
- basis: bfloat16 [8192, 256], replicated, may hold values from -0.0625 to 0.0625
- out_grad: bfloat16 [36864, 14592], P('dp', 'tensor'), may hold values from -0.109375 to 0.109375
- first_moment: float32 [8, 1824, 256], P('tensor', 'dp'), may hold values from -6 to 6
- second_moment: float32 [8, 1824, 256], P('tensor', 'dp'), may hold values from 0.02 to 0.5
Outputs:
- new_first_moment: float32 [8, 1824, 256], P('tensor', 'dp')
- new_second_moment: float32 [8, 1824, 256], P('tensor', 'dp')
- full_update: bfloat16 [8, 1824, 8192], P('tensor', 'dp')
All inputs are finite; a program needn't handle non-finite values.
Results may differ from a plain program's by a relative error of at most 0.005.
Values may be sent and summed in bfloat16 or wider, within the bound.
A program may use at most 32 MiB of HBM per device.

v0:
```python
import jax
import jax.numpy as jnp
from jax import lax
from jax.sharding import PartitionSpec as P

STEP = 100


def gather_rows(coded_local):
    return lax.all_gather(coded_local, "tensor", axis=0, tiled=True)


def owner_total(term):
    return lax.psum_scatter(term, "dp", scatter_dimension=0, tiled=True)


def on_device(activations, basis, out_grad, first_moment, second_moment):
    feat_count = activations.shape[1]
    feat_start = lax.axis_index("tensor") * feat_count
    basis_rows = lax.dynamic_slice_in_dim(basis, feat_start, feat_count, 0)
    partial_code = jnp.dot(activations, basis_rows, preferred_element_type=jnp.float32)
    coded_local = lax.psum_scatter(partial_code, "tensor", scatter_dimension=0, tiled=True).astype(
        jnp.bfloat16
    )
    contract = (((0,), (0,)), ((), ()))
    coded_rows = gather_rows(coded_local)
    term = lax.dot_general(out_grad, coded_rows, contract, preferred_element_type=jnp.float32)
    coded_grad = owner_total(term)
    coded_grad = coded_grad[None]
    new_first = 0.9 * first_moment + 0.1 * coded_grad
    new_second = 0.999 * second_moment + 0.001 * coded_grad * coded_grad
    first_hat = new_first / (1.0 - 0.9**STEP)
    second_hat = new_second / (1.0 - 0.999**STEP)
    direction = (first_hat / (jnp.sqrt(second_hat) + 1e-08)).astype(jnp.bfloat16)
    update = lax.dot_general(
        direction[0], basis, (((1,), (1,)), ((), ())), preferred_element_type=jnp.float32
    )
    return (new_first, new_second, update.astype(jnp.bfloat16)[None])


def solution(mesh):
    placed = (
        P("dp", "tensor"),
        P(),
        P("dp", "tensor"),
        P("tensor", "dp", None),
        P("tensor", "dp", None),
    )
    return jax.shard_map(
        on_device,
        mesh=mesh,
        in_specs=placed,
        out_specs=(P("tensor", "dp", None), P("tensor", "dp", None), P("tensor", "dp", None)),
        check_vma=False,
    )
```

profile of v0, /device:TPU:2, one launch (start us, length us, event | category | flops | bytes accessed | tf_op | source)
XLA Modules:
  0.0 427.0 jit_solution(8018573441105323798)
XLA Ops:
  7.2 0.0 copy-start
  7.2 0.0 reduce-scatter.6.cloned.1.call-start
  7.2 1.9 convolution_bitcast_fusion.1
  9.1 0.9 copy.22
  10.0 0.0 reduce-scatter.6.cloned.1.call-update
  10.0 51.0 %reduce-scatter.6.cloned.1.call-done = f32[48,256]{1,0:T(8,128)} async-done(((f32[384,256]{1,0:T(8,128)}), f32[48,256]{1,0:T(8,128)}) %reduce-scatter.6.cloned.1.call-update) | async-done | bytes 49168 | tf_op jit(solution)/shard_map/reduce_scatter | solution.py:22
  61.0 0.8 convert_element_type.9
  61.8 14.6 %all_gather.3 = bf16[384,256]{1,0:T(8,128)(2,1)S(1)} all-gather(bf16[48,256]{1,0:T(8,128)(2,1)S(1)} %convert_element_type.9), channel_id=1, replica_groups=mesh['dp'=96,'tensor'=8] {'tensor'}, dimensions={0}, use_global_device_ids=true | all-gather | bytes 221184 | tf_op jit(solution)/shard_map/all_gather | solution.py:10
  76.5 0.6 convolution_bitcast_fusion
  77.1 0.0 copy-start.1
  77.1 0.0 copy-start.2
  77.1 217.4 %fusion = f32[24,256]{1,0:T(8,128)S(1)} fusion(f32[1824,256]{1,0:T(8,128)S(1)} %convolution_bitcast_fusion), kind=kCustom, calls=%all-reduce-scatter | all-reduce-scatter fusion | flops 589825 | bytes 1896448
  294.6 1.9 collective-permute-start
  296.5 1.9 collective-permute-start.1
  298.4 1.9 collective-permute-start.10
  300.3 12.7 %collective-permute-start.11 = (f32[24,256]{1,0:T(8,128)S(1)}, f32[24,256]{1,0:T(8,128)S(1)}, u32[]{:S(2)}, u32[]{:S(2)}) collective-permute-start(f32[24,256]{1,0:T(8,128)S(1)} %fusion), channel_id=1, source_target_pairs={{0,96},{8,104},{16,112},{24,120},{32,128},{40,136},{48,144},{56,15... | collective-permute-start | bytes 73736
  313.1 1.9 collective-permute-start.19
  315.0 13.3 %collective-permute-done.19 = f32[19,256]{1,0:T(8,128)S(1)} collective-permute-done((f32[19,256]{1,0:T(8,128)S(1)}, f32[19,256]{1,0:T(8,128)S(1)}, u32[]{:S(2)}, u32[]{:S(2)}) %collective-permute-start.19) | collective-permute-done | bytes 19488
  328.4 1.9 collective-permute-start.12
  330.3 26.8 %collective-permute-start.13 = (f32[24,256]{1,0:T(8,128)S(1)}, f32[24,256]{1,0:T(8,128)S(1)}, u32[]{:S(2)}, u32[]{:S(2)}) collective-permute-start(f32[24,256]{1,0:T(8,128)S(1)} %fusion), channel_id=1, source_target_pairs={{0,112},{8,120},{16,128},{24,136},{32,144},{40,152},{48,160},{56,1... | collective-permute-start | bytes 73736
  357.1 3.1 collective-permute-start.14
  360.2 6.6 %collective-permute-start.15 = (f32[24,256]{1,0:T(8,128)S(1)}, f32[24,256]{1,0:T(8,128)S(1)}, u32[]{:S(2)}, u32[]{:S(2)}) collective-permute-start(f32[24,256]{1,0:T(8,128)S(1)} %fusion), channel_id=1, source_target_pairs={{0,128},{8,136},{16,144},{24,152},{32,160},{40,168},{48,176},{56,1... | collective-permute-start | bytes 73736
  366.8 2.8 collective-permute-start.16
  369.7 1.9 collective-permute-start.17
  371.6 0.0 collective-permute-done.13
  371.6 1.9 collective-permute-start.18
  373.5 0.0 collective-permute-done.14
  373.5 3.4 collective-permute-start.2
  376.9 0.0 collective-permute-done.15
  376.9 4.0 collective-permute-start.3
  380.9 0.0 collective-permute-done.16
  380.9 3.5 collective-permute-start.4
  384.4 0.0 collective-permute-done.17
  384.4 3.0 collective-permute-start.5
  387.4 0.0 collective-permute-done.18
  387.4 4.4 %collective-permute-start.6 = (f32[24,256]{1,0:T(8,128)S(1)}, f32[24,256]{1,0:T(8,128)S(1)}, u32[]{:S(2)}, u32[]{:S(2)}) collective-permute-start(f32[24,256]{1,0:T(8,128)S(1)} %fusion), channel_id=1, source_target_pairs={{0,56},{8,64},{16,72},{24,80},{32,88},{40,96},{48,104},{56,112},{6... | collective-permute-start | bytes 73736
  391.8 3.0 collective-permute-start.7
  394.8 4.5 %collective-permute-start.8 = (f32[24,256]{1,0:T(8,128)S(1)}, f32[24,256]{1,0:T(8,128)S(1)}, u32[]{:S(2)}, u32[]{:S(2)}) collective-permute-start(f32[24,256]{1,0:T(8,128)S(1)} %fusion), channel_id=1, source_target_pairs={{0,72},{8,80},{16,88},{24,96},{32,104},{40,112},{48,120},{56,128},... | collective-permute-start | bytes 73736
  399.4 0.0 collective-permute-done.4
  399.4 4.0 collective-permute-start.9
  403.4 1.3 dynamic-slice.4
  405.3 0.0 collective-permute-done.6
  405.3 3.3 collective-permute-done.8
  408.6 3.4 collective-permute-done.9
  412.0 2.7 concatenate
  414.7 0.6 copy.20
  415.4 4.1 fusion.1
  419.5 0.6 copy.21
  (14 shorter events, 0.1 us)
Async XLA Ops:
  7.2 69.3 %copy-start = (bf16[384,1824]{0,1:T(8,128)(2,1)S(1)}, bf16[384,1824]{0,1:T(8,128)(2,1)}, u32[]{:S(2)}) copy-start(bf16[384,1824]{0,1:T(8,128)(2,1)} %param.7) | copy-start | bytes 4202500
  7.2 53.8 %reduce-scatter.6.cloned.1.call-start = ((), (), s32[]{:S(2)}) async-start(), calls=%async_computation.1 | async-start | bytes 442368 | tf_op jit(solution)/shard_map/reduce_scatter | solution.py:22
  77.1 337.6 %copy-start.1 = (f32[1,19,256]{2,0,1:T(1,128)S(1)}, f32[1,19,256]{2,0,1:T(1,128)}, u32[]{:S(2)}) copy-start(f32[1,19,256]{2,0,1:T(1,128)} %param.9) | copy-start | bytes 58372
  77.1 337.6 %copy-start.2 = (f32[1,19,256]{2,0,1:T(1,128)S(1)}, f32[1,19,256]{2,0,1:T(1,128)}, u32[]{:S(2)}) copy-start(f32[1,19,256]{2,0,1:T(1,128)} %param.8) | copy-start | bytes 58372
  294.6 35.7 %collective-permute-start = (f32[24,256]{1,0:T(8,128)S(1)}, f32[24,256]{1,0:T(8,128)S(1)}, u32[]{:S(2)}, u32[]{:S(2)}) collective-permute-start(f32[24,256]{1,0:T(8,128)S(1)} %fusion), channel_id=1, source_target_pairs={{0,8},{8,16},{16,24},{24,32},{32,40},{40,48},{48,56},{56,64},{64,7... | collective-permute-start | bytes 73736
  296.5 60.6 %collective-permute-start.1 = (f32[24,256]{1,0:T(8,128)S(1)}, f32[24,256]{1,0:T(8,128)S(1)}, u32[]{:S(2)}, u32[]{:S(2)}) collective-permute-start(f32[24,256]{1,0:T(8,128)S(1)} %fusion), channel_id=1, source_target_pairs={{0,16},{8,24},{16,32},{24,40},{32,48},{40,56},{48,64},{56,72},{64,... | collective-permute-start | bytes 73736
  298.4 61.7 %collective-permute-start.10 = (f32[24,256]{1,0:T(8,128)S(1)}, f32[24,256]{1,0:T(8,128)S(1)}, u32[]{:S(2)}, u32[]{:S(2)}) collective-permute-start(f32[24,256]{1,0:T(8,128)S(1)} %fusion), channel_id=1, source_target_pairs={{0,88},{8,96},{16,104},{24,112},{32,120},{40,128},{48,136},{56,144... | collective-permute-start | bytes 73736
  300.3 66.5 %collective-permute-start.11 = (f32[24,256]{1,0:T(8,128)S(1)}, f32[24,256]{1,0:T(8,128)S(1)}, u32[]{:S(2)}, u32[]{:S(2)}) collective-permute-start(f32[24,256]{1,0:T(8,128)S(1)} %fusion), channel_id=1, source_target_pairs={{0,96},{8,104},{16,112},{24,120},{32,128},{40,136},{48,144},{56,15... | collective-permute-start | bytes 73736
  313.1 15.3 %collective-permute-start.19 = (f32[19,256]{1,0:T(8,128)S(1)}, f32[19,256]{1,0:T(8,128)S(1)}, u32[]{:S(2)}, u32[]{:S(2)}) collective-permute-start(f32[19,256]{1,0:T(8,128)S(1)} %slice), channel_id=1, source_target_pairs={{0,160},{8,168},{16,176},{24,184},{32,192},{40,200},{48,208},{56,2... | collective-permute-start | bytes 58376
  328.4 41.3 %collective-permute-start.12 = (f32[24,256]{1,0:T(8,128)S(1)}, f32[24,256]{1,0:T(8,128)S(1)}, u32[]{:S(2)}, u32[]{:S(2)}) collective-permute-start(f32[24,256]{1,0:T(8,128)S(1)} %fusion), channel_id=1, source_target_pairs={{0,104},{8,112},{16,120},{24,128},{32,136},{40,144},{48,152},{56,1... | collective-permute-start | bytes 73736
  330.3 41.3 %collective-permute-start.13 = (f32[24,256]{1,0:T(8,128)S(1)}, f32[24,256]{1,0:T(8,128)S(1)}, u32[]{:S(2)}, u32[]{:S(2)}) collective-permute-start(f32[24,256]{1,0:T(8,128)S(1)} %fusion), channel_id=1, source_target_pairs={{0,112},{8,120},{16,128},{24,136},{32,144},{40,152},{48,160},{56,1... | collective-permute-start | bytes 73736
  357.1 16.5 %collective-permute-start.14 = (f32[24,256]{1,0:T(8,128)S(1)}, f32[24,256]{1,0:T(8,128)S(1)}, u32[]{:S(2)}, u32[]{:S(2)}) collective-permute-start(f32[24,256]{1,0:T(8,128)S(1)} %fusion), channel_id=1, source_target_pairs={{0,120},{8,128},{16,136},{24,144},{32,152},{40,160},{48,168},{56,1... | collective-permute-start | bytes 73736
  360.2 16.8 %collective-permute-start.15 = (f32[24,256]{1,0:T(8,128)S(1)}, f32[24,256]{1,0:T(8,128)S(1)}, u32[]{:S(2)}, u32[]{:S(2)}) collective-permute-start(f32[24,256]{1,0:T(8,128)S(1)} %fusion), channel_id=1, source_target_pairs={{0,128},{8,136},{16,144},{24,152},{32,160},{40,168},{48,176},{56,1... | collective-permute-start | bytes 73736
  366.8 14.1 %collective-permute-start.16 = (f32[24,256]{1,0:T(8,128)S(1)}, f32[24,256]{1,0:T(8,128)S(1)}, u32[]{:S(2)}, u32[]{:S(2)}) collective-permute-start(f32[24,256]{1,0:T(8,128)S(1)} %fusion), channel_id=1, source_target_pairs={{0,136},{8,144},{16,152},{24,160},{32,168},{40,176},{48,184},{56,1... | collective-permute-start | bytes 73736
  369.7 14.7 %collective-permute-start.17 = (f32[24,256]{1,0:T(8,128)S(1)}, f32[24,256]{1,0:T(8,128)S(1)}, u32[]{:S(2)}, u32[]{:S(2)}) collective-permute-start(f32[24,256]{1,0:T(8,128)S(1)} %fusion), channel_id=1, source_target_pairs={{0,144},{8,152},{16,160},{24,168},{32,176},{40,184},{48,192},{56,2... | collective-permute-start | bytes 73736
  371.6 15.8 %collective-permute-start.18 = (f32[24,256]{1,0:T(8,128)S(1)}, f32[24,256]{1,0:T(8,128)S(1)}, u32[]{:S(2)}, u32[]{:S(2)}) collective-permute-start(f32[24,256]{1,0:T(8,128)S(1)} %fusion), channel_id=1, source_target_pairs={{0,152},{8,160},{16,168},{24,176},{32,184},{40,192},{48,200},{56,2... | collective-permute-start | bytes 73736
  373.5 18.2 %collective-permute-start.2 = (f32[24,256]{1,0:T(8,128)S(1)}, f32[24,256]{1,0:T(8,128)S(1)}, u32[]{:S(2)}, u32[]{:S(2)}) collective-permute-start(f32[24,256]{1,0:T(8,128)S(1)} %fusion), channel_id=1, source_target_pairs={{0,24},{8,32},{16,40},{24,48},{32,56},{40,64},{48,72},{56,80},{64,... | collective-permute-start | bytes 73736
  376.9 17.9 %collective-permute-start.3 = (f32[24,256]{1,0:T(8,128)S(1)}, f32[24,256]{1,0:T(8,128)S(1)}, u32[]{:S(2)}, u32[]{:S(2)}) collective-permute-start(f32[24,256]{1,0:T(8,128)S(1)} %fusion), channel_id=1, source_target_pairs={{0,32},{8,40},{16,48},{24,56},{32,64},{40,72},{48,80},{56,88},{64,... | collective-permute-start | bytes 73736
  380.9 18.5 %collective-permute-start.4 = (f32[24,256]{1,0:T(8,128)S(1)}, f32[24,256]{1,0:T(8,128)S(1)}, u32[]{:S(2)}, u32[]{:S(2)}) collective-permute-start(f32[24,256]{1,0:T(8,128)S(1)} %fusion), channel_id=1, source_target_pairs={{0,40},{8,48},{16,56},{24,64},{32,72},{40,80},{48,88},{56,96},{64,... | collective-permute-start | bytes 73736
  384.4 20.9 %collective-permute-start.5 = (f32[24,256]{1,0:T(8,128)S(1)}, f32[24,256]{1,0:T(8,128)S(1)}, u32[]{:S(2)}, u32[]{:S(2)}) collective-permute-start(f32[24,256]{1,0:T(8,128)S(1)} %fusion), channel_id=1, source_target_pairs={{0,48},{8,56},{16,64},{24,72},{32,80},{40,88},{48,96},{56,104},{64... | collective-permute-start | bytes 73736
  387.4 17.9 %collective-permute-start.6 = (f32[24,256]{1,0:T(8,128)S(1)}, f32[24,256]{1,0:T(8,128)S(1)}, u32[]{:S(2)}, u32[]{:S(2)}) collective-permute-start(f32[24,256]{1,0:T(8,128)S(1)} %fusion), channel_id=1, source_target_pairs={{0,56},{8,64},{16,72},{24,80},{32,88},{40,96},{48,104},{56,112},{6... | collective-permute-start | bytes 73736
  391.8 13.6 %collective-permute-start.7 = (f32[24,256]{1,0:T(8,128)S(1)}, f32[24,256]{1,0:T(8,128)S(1)}, u32[]{:S(2)}, u32[]{:S(2)}) collective-permute-start(f32[24,256]{1,0:T(8,128)S(1)} %fusion), channel_id=1, source_target_pairs={{0,64},{8,72},{16,80},{24,88},{32,96},{40,104},{48,112},{56,120},{... | collective-permute-start | bytes 73736
  394.8 13.8 %collective-permute-start.8 = (f32[24,256]{1,0:T(8,128)S(1)}, f32[24,256]{1,0:T(8,128)S(1)}, u32[]{:S(2)}, u32[]{:S(2)}) collective-permute-start(f32[24,256]{1,0:T(8,128)S(1)} %fusion), channel_id=1, source_target_pairs={{0,72},{8,80},{16,88},{24,96},{32,104},{40,112},{48,120},{56,128},... | collective-permute-start | bytes 73736
  399.4 12.6 %collective-permute-start.9 = (f32[24,256]{1,0:T(8,128)S(1)}, f32[24,256]{1,0:T(8,128)S(1)}, u32[]{:S(2)}, u32[]{:S(2)}) collective-permute-start(f32[24,256]{1,0:T(8,128)S(1)} %fusion), channel_id=1, source_target_pairs={{0,80},{8,88},{16,96},{24,104},{32,112},{40,120},{48,128},{56,136}... | collective-permute-start | bytes 73736
Sparse Core Ops, SparseCore 0:
  11.7 49.2 reduce-scatter.5
where the time goes:
time: 428 us; the launch traced here: 427 us
  blocking collectives  232 us (54%)
  starting transfers between devices  95.2 us (22%)
  waiting for transfers between devices  71 us (17%)
  between operations  15.1 us (4%)
  matrix products  6.65 us (2%)
  local copies, waits for them, and re-layouts  6.13 us (1%)
    unnamed x1, blocking collectives  217 us
    unnamed x20, starting transfers between devices  95.2 us
    reduce_scatter x1, waiting for transfers between devices, on_device(): lax.psum_scatter(partial_code, 'tensor', scatter_dimension=0, tiled=True)  51 us
    unnamed x21, waiting for transfers between devices  20.1 us
    all_gather x1, blocking collectives, gather_rows(): return lax.all_gather(coded_local, 'tensor', axis=0, tiled=True)  14.6 us
  transfers between devices with their start and end apart: 21, of which 4 were waited for; matrix products, arithmetic and copies ran while one was open for 0% of the time, Pallas kernels for 0%

commit v1 on v0

v1 whole, which is shorter than its diff:
```python
import functools

import jax
import jax.numpy as jnp
from jax import lax
from jax.experimental import pallas as pl
from jax.experimental.pallas import tpu as pltpu
from jax.sharding import PartitionSpec as P

STEP = 100
MESH = pl.DeviceIdType.MESH
F32 = jnp.float32
BF16 = jnp.bfloat16

NX, NZ, NY = 4, 12, 2
NYH, NC = 4, 2
OWN = 19
PAD = 20
PAIRS = NZ // 2
TOK = 48

TENSOR_PEERS = ((2, 0), (2, 1), (1, 0), (3, 0), (1, 1), (3, 1), (0, 1))
XY_PEERS = ((2, 1), (2, 0), (1, 1), (3, 1), (1, 0), (3, 0), (0, 1))
PAIR_STEPS = (3, 2, 4, 1, 5, 0)


def kernel(
    act_hbm, basis_hbm, og_hbm, m_hbm, v_hbm,
    m_out, v_out, upd_out,
    act, rows, basis, og, m_in, v_in,
    part, part_in, code, ogp, chunk, chunk_in, acc, cut, zsend, zin, m_s, v_s,
    load_sem, a_send, a_recv, g_send, g_recv, x_send, x_recv, z_send, z_recv,
):
    dp, t = lax.axis_index("dp"), lax.axis_index("tensor")
    x, z, y = dp // (NZ * NY), lax.rem(dp // NY, NZ), lax.rem(dp, NY)
    yh, core = t // NC, lax.rem(t, NC)
    half = z // 2
    odd = lax.rem(z, 2)

    def tensor_at(k):
        a, c = TENSOR_PEERS[k]
        return lax.rem(yh + a, NYH) * NC + lax.rem(core + c, NC)

    def xy_at(k):
        dx, dy = XY_PEERS[k]
        return lax.rem(x + dx, NX), lax.rem(y + dy, NY)

    feats = act.shape[1]
    start = pl.multiple_of(t * feats, feats)
    loads = [
        pltpu.make_async_copy(act_hbm, act, load_sem.at[0]),
        pltpu.make_async_copy(basis_hbm.at[pl.ds(start, feats)], rows, load_sem.at[1]),
        pltpu.make_async_copy(og_hbm, og, load_sem.at[2]),
        pltpu.make_async_copy(m_hbm, m_in, load_sem.at[3]),
        pltpu.make_async_copy(v_hbm, v_in, load_sem.at[4]),
        pltpu.make_async_copy(basis_hbm, basis, load_sem.at[5]),
    ]
    for load in loads:
        load.start()

    barrier = pltpu.get_barrier_semaphore()
    n_peers = 0
    for dz in range(1, NZ):
        peer = (x * NZ + lax.rem(z + dz, NZ)) * NY + y
        pl.semaphore_signal(barrier, inc=1, device_id=(peer, t), device_id_type=MESH)
        n_peers += 1
    for k in range(len(TENSOR_PEERS)):
        pl.semaphore_signal(barrier, inc=1, device_id=(dp, tensor_at(k)), device_id_type=MESH)
        n_peers += 1
    for k in range(len(XY_PEERS)):
        px, py = xy_at(k)
        peer = (px * NZ + z) * NY + py
        pl.semaphore_signal(barrier, inc=1, device_id=(peer, t), device_id_type=MESH)
        n_peers += 1

    loads[0].wait()
    loads[1].wait()
    coded = jnp.dot(act[...], rows[...], preferred_element_type=F32)
    part[...] = coded.astype(BF16).reshape(part.shape)
    pl.semaphore_wait(barrier, n_peers)

    a_copies = []
    for k in range(len(TENSOR_PEERS)):
        peer = tensor_at(k)
        copy = pltpu.make_async_remote_copy(
            src_ref=part.at[peer], dst_ref=part_in.at[k], send_sem=a_send.at[k], recv_sem=a_recv.at[k],
            device_id=(dp, peer), device_id_type=MESH,
        )
        copy.start()
        a_copies.append(copy)

    loads[2].wait()
    n_out, n_in = 16 * PAD, 16 * OWN
    r = lax.broadcasted_iota(jnp.int32, (n_out, n_in), 0)
    c = lax.broadcasted_iota(jnp.int32, (n_out, n_in), 1)
    quad, in_quad = r // (4 * PAD), lax.rem(r, 4 * PAD)
    place, line = in_quad // PAD, lax.rem(in_quad, PAD)
    owner = quad * 4 + lax.rem(place, 2) * 2 + place // 2
    pick = jnp.where((line < OWN) & (c == owner * OWN + line), 1.0, 0.0).astype(BF16)
    for b in range(NX * NZ * NY // 16):
        moved = jnp.dot(pick, og[b * n_in : (b + 1) * n_in, :], preferred_element_type=F32).astype(BF16)
        for i in range(4):
            ox, oq = (4 * b + i) // PAIRS, (4 * b + i) % PAIRS
            ogp[oq, ox * 4 * PAD : (ox + 1) * 4 * PAD, :] = moved[i * 4 * PAD : (i + 1) * 4 * PAD, :]

    loads[3].wait()
    loads[4].wait()
    m_s[...] = jnp.zeros_like(m_s)
    v_s[...] = jnp.ones_like(v_s)
    for i in range(OWN):
        m_s[i : i + 1, :] = m_in[i]
        v_s[i : i + 1, :] = v_in[i]
    cut[...] = jnp.zeros_like(cut)

    total = part[t].astype(F32)
    for k in range(len(TENSOR_PEERS)):
        a_copies[k].wait_recv()
        total = total + part_in[k].astype(F32)
    code[t] = total.astype(BF16)
    g_copies = []
    for k in range(len(TENSOR_PEERS)):
        peer = tensor_at(k)
        copy = pltpu.make_async_remote_copy(
            src_ref=code.at[t], dst_ref=code.at[t], send_sem=g_send.at[k], recv_sem=g_recv.at[k],
            device_id=(dp, peer), device_id_type=MESH,
        )
        copy.start()
        g_copies.append(copy)
    for copy in g_copies:
        copy.wait_recv()

    coded = code[...].reshape(len(TENSOR_PEERS) * TOK + TOK, code.shape[2])
    x_copies = []
    for j, ahead in enumerate(PAIR_STEPS):
        q = lax.rem(half + ahead, PAIRS)
        term = jnp.dot(ogp[q], coded, preferred_element_type=F32)
        for s in range(NX * NY):
            piece = term[s * 2 * PAD : (s + 1) * 2 * PAD, :]
            chunk[j, s] = jnp.concatenate([piece[:, :128], piece[:, 128:]], axis=0).astype(BF16)
        for k in range(len(XY_PEERS)):
            px, py = xy_at(k)
            copy = pltpu.make_async_remote_copy(
                src_ref=chunk.at[j, px * NY + py], dst_ref=chunk_in.at[j, k],
                send_sem=x_send.at[j, k], recv_sem=x_recv.at[j, k],
                device_id=((px * NZ + z) * NY + py, t), device_id_type=MESH,
            )
            copy.start()
            x_copies.append(copy)

    z_copies = []
    for j, ahead in enumerate(PAIR_STEPS):
        q = lax.rem(half + ahead, PAIRS)
        total = chunk[j, x * NY + y].astype(F32)
        for k in range(len(XY_PEERS)):
            x_copies[j * len(XY_PEERS) + k].wait_recv()
            total = total + chunk_in[j, k].astype(F32)
        acc[...] = total
        for zz in range(2):
            cut[zz, 0:PAD, :] = acc[zz * PAD : (zz + 1) * PAD, :]
            cut[zz, 24 : 24 + PAD, :] = acc[(2 + zz) * PAD : (3 + zz) * PAD, :]
            zsend[j, zz] = cut[zz].astype(BF16)
        which = (0, 1) if ahead else (1 - odd,)
        for zz in which:
            peer = (x * NZ + 2 * q + zz) * NY + y
            at = 2 * j + odd if ahead else 2 * j
            copy = pltpu.make_async_remote_copy(
                src_ref=zsend.at[j, zz], dst_ref=zin.at[at],
                send_sem=z_send.at[len(z_copies)], recv_sem=z_recv.at[at],
                device_id=(peer, t), device_id_type=MESH,
            )
            copy.start()
            z_copies.append(copy)

    total = zsend[PAIRS - 1, odd].astype(F32)
    for i in range(NZ - 1):
        pltpu.make_async_copy(zin.at[i], zin.at[i], z_recv.at[i]).wait()
        total = total + zin[i].astype(F32)
    grad = jnp.concatenate([total[0:24], total[24:48]], axis=1)

    new_first = 0.9 * m_s[...] + 0.1 * grad
    new_second = 0.999 * v_s[...] + 0.001 * grad * grad
    first_hat = new_first / (1.0 - 0.9**STEP)
    second_hat = new_second / (1.0 - 0.999**STEP)
    direction = first_hat / (jnp.sqrt(second_hat) + 1e-08)
    direction = jnp.concatenate([direction, jnp.zeros((8, direction.shape[1]), F32)], axis=0).astype(BF16)
    for i in range(OWN):
        m_out[i] = new_first[i : i + 1, :]
        v_out[i] = new_second[i : i + 1, :]
    loads[5].wait()
    wide = 1024
    for i in range(basis.shape[0] // wide):
        upd = lax.dot_general(
            direction, basis[i * wide : (i + 1) * wide, :], (((1,), (1,)), ((), ())), preferred_element_type=F32
        )
        upd_out[:, i * wide : (i + 1) * wide] = upd[:OWN].astype(BF16)
    for copy in a_copies + g_copies + x_copies + z_copies:
        copy.wait_send()


def on_device(activations, basis, out_grad, first_moment, second_moment):
    d, rank = basis.shape
    tokens, feats = activations.shape
    units = out_grad.shape[1]
    any_spec = pl.BlockSpec(memory_space=pl.ANY)
    vmem_spec = pl.BlockSpec(memory_space=pltpu.VMEM)
    dma = pltpu.SemaphoreType.DMA
    n_ten, n_xy = len(TENSOR_PEERS), len(XY_PEERS)
    new_first, new_second, update = pl.pallas_call(
        kernel,
        out_shape=(
            jax.ShapeDtypeStruct((OWN, 1, rank), F32),
            jax.ShapeDtypeStruct((OWN, 1, rank), F32),
            jax.ShapeDtypeStruct((OWN, d), BF16),
        ),
        in_specs=[any_spec] * 5,
        out_specs=(vmem_spec, vmem_spec, vmem_spec),
        scratch_shapes=[
            pltpu.VMEM((tokens, feats), BF16),
            pltpu.VMEM((feats, rank), BF16),
            pltpu.VMEM((d, rank), BF16),
            pltpu.VMEM((units, tokens), BF16),
            pltpu.VMEM((OWN, 1, rank), F32),
            pltpu.VMEM((OWN, 1, rank), F32),
            pltpu.VMEM((n_ten + 1, TOK, rank), BF16),
            pltpu.VMEM((n_ten, TOK, rank), BF16),
            pltpu.VMEM((n_ten + 1, TOK, rank), BF16),
            pltpu.VMEM((PAIRS, NX * NY * 2 * PAD, tokens), BF16),
            pltpu.VMEM((PAIRS, NX * NY, 4 * PAD, 128), BF16),
            pltpu.VMEM((PAIRS, n_xy, 4 * PAD, 128), BF16),
            pltpu.VMEM((4 * PAD, 128), F32),
            pltpu.VMEM((2, 48, 128), F32),
            pltpu.VMEM((PAIRS, 2, 48, 128), BF16),
            pltpu.VMEM((NZ - 1, 48, 128), BF16),
            pltpu.VMEM((24, rank), F32),
            pltpu.VMEM((24, rank), F32),
            dma((6,)),
            dma((n_ten,)),
            dma((n_ten,)),
            dma((n_ten,)),
            dma((n_ten,)),
            dma((PAIRS, n_xy)),
            dma((PAIRS, n_xy)),
            dma((NZ - 1,)),
            dma((NZ - 1,)),
        ],
        compiler_params=pltpu.CompilerParams(
            collective_id=0, has_side_effects=True, vmem_limit_bytes=60 << 20
        ),
        name="galore_step",
    )(
        activations,
        basis,
        out_grad.T,
        first_moment.transpose(1, 0, 2),
        second_moment.transpose(1, 0, 2),
    )
    return new_first.transpose(1, 0, 2), new_second.transpose(1, 0, 2), update[None]


def solution(mesh):
    placed = (
        P("dp", "tensor"),
        P(),
        P("dp", "tensor"),
        P("tensor", "dp", None),
        P("tensor", "dp", None),
    )
    return jax.shard_map(
        on_device,
        mesh=mesh,
        in_specs=placed,
        out_specs=(P("tensor", "dp", None), P("tensor", "dp", None), P("tensor", "dp", None)),
        check_vma=False,
    )
```

time: 428 us -> 56.5 us (0.13)
  the two profiles are of different devices: /device:TPU:2 before, /device:TPU:1 now
where the time goes in v1:
time: 56.5 us; the launch traced here: 56.2 us
  Pallas kernels  51.1 us (90%)
  local copies, waits for them, and re-layouts  4.43 us (8%)
  between operations  0.64 us (1%)
    pallas_call x1, Pallas kernels, on_device(): pl.pallas_call(kernel, out_shape=(jax.ShapeDtypeStruct((OWN, 1, rank), F3...  51.1 us
    unnamed x3, local copies, waits for them, and re-layouts  4.43 us

profile of v1, /device:TPU:1, one launch (start us, length us, event | category | flops | bytes accessed | tf_op | source)
XLA Modules:
  0.0 56.2 jit_solution(15596996462097592936)
XLA Ops:
  0.6 51.1 %galore_step.1 = (f32[19,1,256]{2,1,0:T(1,128)}, f32[19,1,256]{2,1,0:T(1,128)}, bf16[19,8192]{1,0:T(8,128)(2,1)}) custom-call(bf16[384,1024]{1,0:T(8,128)(2,1)} %act_hbm.1, bf16[8192,256]{1,0:T(8,128)(2,1)} %basis_hbm.1, bf16[1824,384]{1,0:T(8,128)(2,1)} %bitcast.6, f32[19,1,256]{2,1,0:T(1,128)} %bitcast.8, f32[19,1,256]{2,1,0:T(1,128)} %bitcast.9), custom_call_target="tpu_custom_call" | custom-call | tf_op jit(solution)/shard_map/galore_step/pallas_call | solution.py:208
  51.8 1.3 %copy.11 = f32[1,19,256]{2,0,1:T(1,128)} copy(f32[1,19,256]{2,0,1:T(1,128)} %bitcast.11) | data formatting | bytes 38912
  53.1 1.3 %copy.12 = f32[1,19,256]{2,0,1:T(1,128)} copy(f32[1,19,256]{2,0,1:T(1,128)} %bitcast.10) | data formatting | bytes 38912
  54.5 1.8 %copy.13 = bf16[1,19,8192]{2,1,0:T(8,128)(2,1)} copy(bf16[1,19,8192]{2,1,0:T(8,128)(2,1)} %bitcast.7) | data formatting | bytes 622592

commit v2 on v0

v2 whole, which is shorter than its diff:
```python
import functools

import jax
import jax.numpy as jnp
from jax import lax
from jax.experimental import pallas as pl
from jax.experimental.pallas import tpu as pltpu
from jax.sharding import PartitionSpec as P

STEP = 100
MESH = pl.DeviceIdType.MESH
F32 = jnp.float32
BF16 = jnp.bfloat16

NX, NZ, NY = 4, 12, 2
NYH, NC = 4, 2
OWN = 19
PAD = 20
QUADS = NZ // 4
TOK = 48
HALF = 128

TENSOR_PEERS = ((2, 0), (2, 1), (1, 0), (3, 0), (1, 1), (3, 1), (0, 1))
XY_PEERS = ((2, 0), (1, 1), (3, 1), (1, 0), (3, 0), (0, 1))
FAR_PEER = (2, 1)
QUAD_STEPS = (1, 2, 0)


def reduce_kernel(
    act_hbm, basis_hbm, og_hbm, m_hbm, v_hbm,
    grad_out, turned_out, m_out, v_out,
    act, rows, basis, og, m_in, v_in,
    part, part_in, code, ogp, chunk, chunk_in, acc, far_acc, far_send, far_in, far_sum, far_got, near_acc, near_send, near_in,
    load_sem, a_send, a_recv, g_send, g_recv, x_send, x_recv, f_send, f_recv, l_send, l_recv, z_send, z_recv,
):
    dp, t = lax.axis_index("dp"), lax.axis_index("tensor")
    x, z, y = dp // (NZ * NY), lax.rem(dp // NY, NZ), lax.rem(dp, NY)
    yh, core = t // NC, lax.rem(t, NC)
    own_quad, own_place = z // 4, lax.rem(z, 4)
    n_ten, n_xy = len(TENSOR_PEERS), len(XY_PEERS)

    def tensor_at(k):
        a, c = TENSOR_PEERS[k]
        return lax.rem(yh + a, NYH) * NC + lax.rem(core + c, NC)

    def xy_at(k):
        dx, dy = XY_PEERS[k]
        return lax.rem(x + dx, NX), lax.rem(y + dy, NY)

    def dp_at(px, pz, py):
        return (lax.rem(px, NX) * NZ + lax.rem(pz, NZ)) * NY + lax.rem(py, NY)

    barrier = pltpu.get_barrier_semaphore()

    def signal(to_dp, to_t):
        pl.semaphore_signal(barrier, inc=1, device_id=(to_dp, to_t), device_id_type=MESH)

    for dz in (6, 5, 7, 4, 8, 3, 9, 2, 10, 1, 11):
        signal(dp_at(x, z + dz, y), t)
    for k in range(n_ten):
        signal(dp, tensor_at(k))
    far_dp = dp_at(x + FAR_PEER[0], z, y + FAR_PEER[1])
    signal(far_dp, t)
    for dx, dy in XY_PEERS:
        signal(dp_at(x + dx, z, y + dy), t)

    tokens, feats = act.shape
    start = pl.multiple_of(t * feats, feats)
    n_cut = 4
    first_loads = []
    for i in range(n_cut):
        n = feats // n_cut
        first_loads.append(
            pltpu.make_async_copy(
                basis_hbm.at[pl.ds(start + i * n, n)], rows.at[pl.ds(i * n, n)], load_sem.at[i]
            )
        )
        n = tokens // n_cut
        first_loads.append(
            pltpu.make_async_copy(
                act_hbm.at[pl.ds(i * n, n)], act.at[pl.ds(i * n, n)], load_sem.at[n_cut + i]
            )
        )
    og_load = pltpu.make_async_copy(og_hbm, og, load_sem.at[2 * n_cut])
    m_load = pltpu.make_async_copy(m_hbm, m_in, load_sem.at[2 * n_cut + 1])
    v_load = pltpu.make_async_copy(v_hbm, v_in, load_sem.at[2 * n_cut + 2])
    basis_load = pltpu.make_async_copy(basis_hbm, basis, load_sem.at[2 * n_cut + 3])
    for load in first_loads:
        load.start()

    for load in first_loads:
        load.wait()
    og_load.start()
    m_load.start()
    v_load.start()
    basis_load.start()
    a_copies = []
    for h in range(2):
        coded = jnp.dot(act[...], rows[:, h * HALF : (h + 1) * HALF], preferred_element_type=F32)
        part[h] = coded.astype(BF16).reshape(part.shape[1:])
        if h == 0:
            pl.semaphore_wait(barrier, NZ - 1 + n_ten + 1 + n_xy)
        for k in range(n_ten):
            peer = tensor_at(k)
            copy = pltpu.make_async_remote_copy(
                src_ref=part.at[h, peer], dst_ref=part_in.at[h, k],
                send_sem=a_send.at[h, k], recv_sem=a_recv.at[h, k],
                device_id=(dp, peer), device_id_type=MESH,
            )
            copy.start()
            a_copies.append(copy)

    og_load.wait()
    n_out, n_in = 16 * PAD, 16 * OWN
    unit_rows = 8 * PAD
    r = lax.broadcasted_iota(jnp.int32, (n_out, n_in), 0)
    c = lax.broadcasted_iota(jnp.int32, (n_out, n_in), 1)
    unit, in_unit = r // unit_rows, lax.rem(r, unit_rows)
    place, line = in_unit // PAD, lax.rem(in_unit, PAD)
    owner = unit * 8 + lax.rem(place, 4) * 2 + place // 4
    pick = jnp.where((line < OWN) & (c == owner * OWN + line), 1.0, 0.0).astype(BF16)
    for b in range(NX * NZ * NY // 16):
        moved = jnp.dot(pick, og[b * n_in : (b + 1) * n_in, :], preferred_element_type=F32).astype(BF16)
        for i in range(2):
            ox, oq = (2 * b + i) // QUADS, (2 * b + i) % QUADS
            ogp[oq, ox * unit_rows : (ox + 1) * unit_rows, :] = moved[i * unit_rows : (i + 1) * unit_rows, :]
    far_acc[...] = jnp.zeros_like(far_acc)
    near_acc[...] = jnp.zeros_like(near_acc)

    g_copies = []
    for h in range(2):
        total = part[h, t].astype(F32)
        for k in range(n_ten):
            a_copies[h * n_ten + k].wait_recv()
            total = total + part_in[h, k].astype(F32)
        code[h, t] = total.astype(BF16)
        for k in range(n_ten):
            copy = pltpu.make_async_remote_copy(
                src_ref=code.at[h, t], dst_ref=code.at[h, t],
                send_sem=g_send.at[h, k], recv_sem=g_recv.at[h, k],
                device_id=(dp, tensor_at(k)), device_id_type=MESH,
            )
            copy.start()
            g_copies.append(copy)

    m_load.wait()
    v_load.wait()
    m_out[...] = jnp.zeros_like(m_out)
    v_out[...] = jnp.ones_like(v_out)
    for i in range(OWN):
        m_out[i : i + 1, :] = m_in[i]
        v_out[i : i + 1, :] = v_in[i]
    basis_load.wait()
    wide = 1024
    for i in range(basis.shape[0] // wide):
        turned_out[:, i * wide : (i + 1) * wide] = basis[i * wide : (i + 1) * wide, :].T

    def along_z(src, dst, send_sem, recv_sem):
        copies = []
        for j, ahead in enumerate(QUAD_STEPS):
            copies.append([])
            for e in range(0 if ahead else 1, 4):
                zz = e if ahead else lax.rem(own_place + e, 4)
                to = 4 * lax.rem(own_quad + ahead, QUADS) + zz
                slot = lax.rem(to - z + NZ, NZ) - 1
                copies[j].append(
                    pltpu.make_async_remote_copy(
                        src_ref=src.at[j, zz], dst_ref=dst.at[slot],
                        send_sem=send_sem.at[4 * j + e - (not ahead)], recv_sem=recv_sem.at[slot],
                        device_id=((x * NZ + to) * NY + y, t), device_id_type=MESH,
                    )
                )
        return copies

    def sum_along_z(src, dst, recv_sem):
        total = src[QUADS - 1, own_place].astype(F32)
        for i in range(NZ - 1):
            pltpu.make_async_copy(dst.at[i], dst.at[i], recv_sem.at[i]).wait()
            total = total + dst[i].astype(F32)
        return total

    far_copies = along_z(far_send, far_in, f_send, f_recv)
    near_copies = along_z(near_send, near_in, z_send, z_recv)
    far_place = lax.rem(x + FAR_PEER[0], NX) * NY + lax.rem(y + FAR_PEER[1], NY)
    far_rows = pl.ds(pl.multiple_of(far_place * 4 * PAD, 4 * PAD), 4 * PAD)
    x_copies = []
    for h in range(2):
        for k in range(n_ten):
            g_copies[h * n_ten + k].wait_recv()
        coded = code[h].reshape((n_ten + 1) * TOK, HALF)

        def far_part():
            for j, ahead in enumerate(QUAD_STEPS):
                q = lax.rem(own_quad + ahead, QUADS)
                acc[...] = jnp.dot(ogp[q, far_rows, :], coded, preferred_element_type=F32)
                for zz in range(4):
                    far_acc[j, zz, 24 * h : 24 * h + PAD, :] = acc[zz * PAD : (zz + 1) * PAD, :]

        if h == 1:
            far_part()
            for j in range(QUADS):
                for zz in range(4):
                    far_send[j, zz] = far_acc[j, zz].astype(BF16)
                for copy in far_copies[j]:
                    copy.start()
        for j, ahead in enumerate(QUAD_STEPS):
            q = lax.rem(own_quad + ahead, QUADS)
            at = h * QUADS + j
            term = jnp.dot(ogp[q], coded, preferred_element_type=F32)
            chunk[at] = term.astype(BF16).reshape(chunk.shape[1:])
            for k in range(n_xy):
                px, py = xy_at(k)
                copy = pltpu.make_async_remote_copy(
                    src_ref=chunk.at[at, px * NY + py], dst_ref=chunk_in.at[at, k],
                    send_sem=x_send.at[at, k], recv_sem=x_recv.at[at, k],
                    device_id=((px * NZ + z) * NY + py, t), device_id_type=MESH,
                )
                copy.start()
                x_copies.append(copy)
        if h == 0:
            far_part()

    far_copy = pltpu.make_async_remote_copy(
        src_ref=far_sum, dst_ref=far_got, send_sem=l_send, recv_sem=l_recv, device_id=(far_dp, t), device_id_type=MESH
    )
    for h in range(2):
        for j in range(QUADS):
            at = h * QUADS + j
            if at == 2 * QUADS - 1:
                far_sum[...] = sum_along_z(far_send, far_in, f_recv).astype(BF16)
                far_copy.start()
            total = chunk[at, x * NY + y].astype(F32)
            for k in range(n_xy):
                x_copies[at * n_xy + k].wait_recv()
                total = total + chunk_in[at, k].astype(F32)
            acc[...] = total
            for zz in range(4):
                near_acc[j, zz, 24 * h : 24 * h + PAD, :] = acc[zz * PAD : (zz + 1) * PAD, :]
            if h == 1:
                for zz in range(4):
                    near_send[j, zz] = near_acc[j, zz].astype(BF16)
                for copy in near_copies[j]:
                    copy.start()

    total = sum_along_z(near_send, near_in, z_recv)
    far_copy.wait_recv()
    total = total + far_got[...].astype(F32)
    grad_out[...] = jnp.concatenate([total[0:24], total[24:48]], axis=1)
    z_copies = [far_copy] + sum(far_copies + near_copies, [])
    for copy in a_copies + g_copies + x_copies + z_copies:
        copy.wait_send()


def step_kernel(grad, turned, m, v, m_hbm, v_hbm, upd_hbm, m_rows, v_rows, upd, sem):
    g = grad[...]
    new_first = 0.9 * m[...] + 0.1 * g
    new_second = 0.999 * v[...] + 0.001 * g * g
    first_hat = new_first / (1.0 - 0.9**STEP)
    second_hat = new_second / (1.0 - 0.999**STEP)
    direction = first_hat / (jnp.sqrt(second_hat) + 1e-08)
    direction = jnp.concatenate([direction, jnp.zeros((8, direction.shape[1]), F32)], axis=0).astype(BF16)
    wide = 2048
    saves = []
    for i in range(turned.shape[1] // wide):
        cols = pl.ds(i * wide, wide)
        upd[:, cols] = jnp.dot(direction, turned[:, cols], preferred_element_type=F32)[:OWN].astype(BF16)
        save = pltpu.make_async_copy(upd.at[:, cols], upd_hbm.at[:, cols], sem.at[i])
        save.start()
        saves.append(save)
    for i in range(OWN):
        m_rows[i] = new_first[i : i + 1, :]
        v_rows[i] = new_second[i : i + 1, :]
    saves.append(pltpu.make_async_copy(m_rows, m_hbm, sem.at[4]))
    saves.append(pltpu.make_async_copy(v_rows, v_hbm, sem.at[5]))
    saves[-2].start()
    saves[-1].start()
    for save in saves:
        save.wait()


def on_device(activations, basis, out_grad, first_moment, second_moment):
    d, rank = basis.shape
    tokens, feats = activations.shape
    units = out_grad.shape[1]
    hbm = pl.BlockSpec(memory_space=pltpu.HBM)
    vmem = pl.BlockSpec(memory_space=pltpu.VMEM)
    dma = pltpu.SemaphoreType.DMA
    n_ten, n_xy = len(TENSOR_PEERS), len(XY_PEERS)
    steps = 2 * QUADS
    grad, turned, m, v = pl.pallas_call(
        reduce_kernel,
        out_shape=(
            jax.ShapeDtypeStruct((24, rank), F32),
            jax.ShapeDtypeStruct((rank, d), BF16),
            jax.ShapeDtypeStruct((24, rank), F32),
            jax.ShapeDtypeStruct((24, rank), F32),
        ),
        in_specs=[hbm] * 5,
        out_specs=(vmem,) * 4,
        scratch_shapes=[
            pltpu.VMEM((tokens, feats), BF16),
            pltpu.VMEM((feats, rank), BF16),
            pltpu.VMEM((d, rank), BF16),
            pltpu.VMEM((units, tokens), BF16),
            pltpu.VMEM((OWN, 1, rank), F32),
            pltpu.VMEM((OWN, 1, rank), F32),
            pltpu.VMEM((2, n_ten + 1, TOK, HALF), BF16),
            pltpu.VMEM((2, n_ten, TOK, HALF), BF16),
            pltpu.VMEM((2, n_ten + 1, TOK, HALF), BF16),
            pltpu.VMEM((QUADS, NX * NY * 4 * PAD, tokens), BF16),
            pltpu.VMEM((steps, NX * NY, 4 * PAD, HALF), BF16),
            pltpu.VMEM((steps, n_xy, 4 * PAD, HALF), BF16),
            pltpu.VMEM((4 * PAD, HALF), F32),
            pltpu.VMEM((QUADS, 4, 48, HALF), F32),
            pltpu.VMEM((QUADS, 4, 48, HALF), BF16),
            pltpu.VMEM((NZ - 1, 48, HALF), BF16),
            pltpu.VMEM((48, HALF), BF16),
            pltpu.VMEM((48, HALF), BF16),
            pltpu.VMEM((QUADS, 4, 48, HALF), F32),
            pltpu.VMEM((QUADS, 4, 48, HALF), BF16),
            pltpu.VMEM((NZ - 1, 48, HALF), BF16),
            dma((12,)),
            dma((2, n_ten)),
            dma((2, n_ten)),
            dma((2, n_ten)),
            dma((2, n_ten)),
            dma((steps, n_xy)),
            dma((steps, n_xy)),
            dma((NZ - 1,)),
            dma((NZ - 1,)),
            dma,
            dma,
            dma((NZ - 1,)),
            dma((NZ - 1,)),
        ],
        compiler_params=pltpu.CompilerParams(
            collective_id=0, has_side_effects=True, vmem_limit_bytes=40 << 20
        ),
        name="reduce_gradient",
    )(*[
        pltpu.with_memory_space_constraint(a, pltpu.HBM)
        for a in (
            activations,
            basis,
            out_grad.T,
            first_moment.transpose(1, 0, 2),
            second_moment.transpose(1, 0, 2),
        )
    ])
    new_first, new_second, update = pl.pallas_call(
        step_kernel,
        out_shape=(
            jax.ShapeDtypeStruct((OWN, 1, rank), F32),
            jax.ShapeDtypeStruct((OWN, 1, rank), F32),
            jax.ShapeDtypeStruct((OWN, d), BF16),
        ),
        in_specs=[vmem] * 4,
        out_specs=(hbm,) * 3,
        scratch_shapes=[
            pltpu.VMEM((OWN, 1, rank), F32),
            pltpu.VMEM((OWN, 1, rank), F32),
            pltpu.VMEM((OWN, d), BF16),
            dma((6,)),
        ],
        compiler_params=pltpu.CompilerParams(vmem_limit_bytes=16 << 20),
        name="adam_update",
    )(grad, turned, m, v)
    return new_first.transpose(1, 0, 2), new_second.transpose(1, 0, 2), update[None]


def solution(mesh):
    placed = (
        P("dp", "tensor"),
        P(),
        P("dp", "tensor"),
        P("tensor", "dp", None),
        P("tensor", "dp", None),
    )
    return jax.shard_map(
        on_device,
        mesh=mesh,
        in_specs=placed,
        out_specs=(P("tensor", "dp", None), P("tensor", "dp", None), P("tensor", "dp", None)),
        check_vma=False,
    )
```

time: 428 us -> 50.1 us (0.12)
  the two profiles are of different devices: /device:TPU:2 before, /device:TPU:1 now
where the time goes in v2:
time: 50.1 us; the launch traced here: 49.5 us
  Pallas kernels  48.8 us (97%)
  between operations  0.64 us (1%)
    pallas_call x1, Pallas kernels, on_device(): pl.pallas_call(reduce_kernel, out_shape=(jax.ShapeDtypeStruct((24, rank),...  47.3 us
    pallas_call x1, Pallas kernels, on_device(): pl.pallas_call(step_kernel, out_shape=(jax.ShapeDtypeStruct((OWN, 1, rank...  1.52 us

profile of v2, /device:TPU:1, one launch (start us, length us, event | category | flops | bytes accessed | tf_op | source)
XLA Modules:
  0.0 49.5 jit_solution(3854433370570169941)
XLA Ops:
  0.6 47.3 %reduce_gradient.1 = (f32[24,256]{1,0:T(8,128)S(1)}, bf16[256,8192]{1,0:T(8,128)(2,1)S(1)}, f32[24,256]{1,0:T(8,128)S(1)}, f32[24,256]{1,0:T(8,128)S(1)}) custom-call(bf16[384,1024]{1,0:T(8,128)(2,1)} %act_hbm.1, bf16[8192,256]{1,0:T(8,128)(2,1)} %basis_hbm.1, bf16[1824,384]{1,0:T(8,128)(2,1)} %bitcast.6, f32[19,1,256]{2,1,0:T(1,128)} %bitcast.7, ...), custom_call_target="tpu_custom_call" | custom-call | tf_op jit(solution)/shard_map/reduce_gradient/pallas_call | solution.py:290
  48.0 1.5 %adam_update.1 = (f32[19,1,256]{2,1,0:T(1,128)}, f32[19,1,256]{2,1,0:T(1,128)}, bf16[19,8192]{1,0:T(8,128)(2,1)}) custom-call(f32[24,256]{1,0:T(8,128)S(1)} %get-tuple-element.10.grad, bf16[256,8192]{1,0:T(8,128)(2,1)S(1)} %get-tuple-element.11.turned, f32[24,256]{1,0:T(8,128)S(1)} %get-tuple-element.12.m, f32[24,256]{1,0:T(8,128)S(1)} %get-tuple-element.13.v), custom_call_target="tpu_custom_call" | custom-call | tf_op jit(solution)/shard_map/adam_update/pallas_call | solution.py:350

commit v3 on v2

--- a/solution.py
+++ b/solution.py
@@ -23,6 +23,8 @@
 TENSOR_PEERS = ((2, 0), (2, 1), (1, 0), (3, 0), (1, 1), (3, 1), (0, 1))
 XY_PEERS = ((2, 0), (1, 1), (3, 1), (1, 0), (3, 0), (0, 1))
 FAR_PEER = (2, 1)
+MERGED_ROUTES = (((1, 0), (1, 1)), ((3, 0), (3, 1)), ((2, 0), (2, 0)), ((1, 0), (1, 0)), ((3, 0), (3, 0)))
+DIRECT_ROUTES = tuple((p, p) for p in XY_PEERS)
 QUAD_STEPS = (1, 2, 0)
 
 
@@ -30,8 +32,8 @@
     act_hbm, basis_hbm, og_hbm, m_hbm, v_hbm,
     grad_out, turned_out, m_out, v_out,
     act, rows, basis, og, m_in, v_in,
-    part, part_in, code, ogp, chunk, chunk_in, acc, far_acc, far_send, far_in, far_sum, far_got, near_acc, near_send, near_in,
-    load_sem, a_send, a_recv, g_send, g_recv, x_send, x_recv, f_send, f_recv, l_send, l_recv, z_send, z_recv,
+    part, part_in, code, ogp, chunk, chunk_in, merged, acc, far_acc, far_send, far_in, far_sum, far_got, near_acc, near_send, near_in,
+    load_sem, a_send, a_recv, g_send, g_recv, x_send, x_recv, f_send, f_recv, l_send, l_recv, z_send, z_recv, hello,
 ):
     dp, t = lax.axis_index("dp"), lax.axis_index("tensor")
     x, z, y = dp // (NZ * NY), lax.rem(dp // NY, NZ), lax.rem(dp, NY)
@@ -43,8 +45,8 @@
         a, c = TENSOR_PEERS[k]
         return lax.rem(yh + a, NYH) * NC + lax.rem(core + c, NC)
 
-    def xy_at(k):
-        dx, dy = XY_PEERS[k]
+    def xy_at(place):
+        dx, dy = place
         return lax.rem(x + dx, NX), lax.rem(y + dy, NY)
 
     def dp_at(px, pz, py):
@@ -55,10 +57,10 @@
     def signal(to_dp, to_t):
         pl.semaphore_signal(barrier, inc=1, device_id=(to_dp, to_t), device_id_type=MESH)
 
-    for dz in (6, 5, 7, 4, 8, 3, 9, 2, 10, 1, 11):
-        signal(dp_at(x, z + dz, y), t)
     for k in range(n_ten):
         signal(dp, tensor_at(k))
+    for dz in (3, 9, 2, 10, 1, 11):
+        signal(dp_at(x, z + dz, y), t)
     far_dp = dp_at(x + FAR_PEER[0], z, y + FAR_PEER[1])
     signal(far_dp, t)
     for dx, dy in XY_PEERS:
@@ -99,7 +101,11 @@
         coded = jnp.dot(act[...], rows[:, h * HALF : (h + 1) * HALF], preferred_element_type=F32)
         part[h] = coded.astype(BF16).reshape(part.shape[1:])
         if h == 0:
-            pl.semaphore_wait(barrier, NZ - 1 + n_ten + 1 + n_xy)
+            pl.semaphore_wait(barrier, n_ten + 6 + 1 + n_xy)
+            for i, dz in enumerate((3, NZ - 3)):
+                pl.semaphore_signal(
+                    hello.at[i], inc=1, device_id=(dp_at(x, z + dz, y), t), device_id_type=MESH
+                )
         for k in range(n_ten):
             peer = tensor_at(k)
             copy = pltpu.make_async_remote_copy(
@@ -183,7 +189,7 @@
     near_copies = along_z(near_send, near_in, z_send, z_recv)
     far_place = lax.rem(x + FAR_PEER[0], NX) * NY + lax.rem(y + FAR_PEER[1], NY)
     far_rows = pl.ds(pl.multiple_of(far_place * 4 * PAD, 4 * PAD), 4 * PAD)
-    x_copies = []
+    x_copies = [[] for _ in range(2 * QUADS)]
     for h in range(2):
         for k in range(n_ten):
             g_copies[h * n_ten + k].wait_recv()
@@ -198,6 +204,8 @@
 
         if h == 1:
             far_part()
+            for i in range(2):
+                pl.semaphore_wait(hello.at[i], 1)
             for j in range(QUADS):
                 for zz in range(4):
                     far_send[j, zz] = far_acc[j, zz].astype(BF16)
@@ -208,46 +216,58 @@
             at = h * QUADS + j
             term = jnp.dot(ogp[q], coded, preferred_element_type=F32)
             chunk[at] = term.astype(BF16).reshape(chunk.shape[1:])
-            for k in range(n_xy):
-                px, py = xy_at(k)
+            for k, (to, share) in enumerate(DIRECT_ROUTES if h else MERGED_ROUTES):
+                px, py = xy_at(to)
+                sx, sy = xy_at(share)
                 copy = pltpu.make_async_remote_copy(
-                    src_ref=chunk.at[at, px * NY + py], dst_ref=chunk_in.at[at, k],
+                    src_ref=chunk.at[at, sx * NY + sy], dst_ref=chunk_in.at[at, k],
                     send_sem=x_send.at[at, k], recv_sem=x_recv.at[at, k],
                     device_id=((px * NZ + z) * NY + py, t), device_id_type=MESH,
                 )
                 copy.start()
-                x_copies.append(copy)
+                x_copies[at].append(copy)
         if h == 0:
             far_part()
 
     far_copy = pltpu.make_async_remote_copy(
         src_ref=far_sum, dst_ref=far_got, send_sem=l_send, recv_sem=l_recv, device_id=(far_dp, t), device_id_type=MESH
     )
-    for h in range(2):
-        for j in range(QUADS):
+    for j in range(QUADS):
+        total = chunk[j, x * NY + 1 - y].astype(F32)
+        for k in range(2):
+            x_copies[j][k].wait_recv()
+            total = total + chunk_in[j, k].astype(F32)
+        merged[j] = total.astype(BF16)
+        copy = pltpu.make_async_remote_copy(
+            src_ref=merged.at[j], dst_ref=chunk_in.at[j, 5], send_sem=x_send.at[j, 5], recv_sem=x_recv.at[j, 5],
+            device_id=(dp_at(x, z, y + 1), t), device_id_type=MESH,
+        )
+        copy.start()
+        x_copies[j].append(copy)
+    for j in range(QUADS):
+        if j == QUADS - 1:
+            far_sum[...] = sum_along_z(far_send, far_in, f_recv).astype(BF16)
+            far_copy.start()
+        for h in range(2):
             at = h * QUADS + j
-            if at == 2 * QUADS - 1:
-                far_sum[...] = sum_along_z(far_send, far_in, f_recv).astype(BF16)
-                far_copy.start()
             total = chunk[at, x * NY + y].astype(F32)
-            for k in range(n_xy):
-                x_copies[at * n_xy + k].wait_recv()
+            for k in range(0 if h else 2, n_xy):
+                x_copies[at][k].wait_recv()
                 total = total + chunk_in[at, k].astype(F32)
             acc[...] = total
             for zz in range(4):
                 near_acc[j, zz, 24 * h : 24 * h + PAD, :] = acc[zz * PAD : (zz + 1) * PAD, :]
-            if h == 1:
-                for zz in range(4):
-                    near_send[j, zz] = near_acc[j, zz].astype(BF16)
-                for copy in near_copies[j]:
-                    copy.start()
+        for zz in range(4):
+            near_send[j, zz] = near_acc[j, zz].astype(BF16)
+        for copy in near_copies[j]:
+            copy.start()
 
     total = sum_along_z(near_send, near_in, z_recv)
     far_copy.wait_recv()
     total = total + far_got[...].astype(F32)
     grad_out[...] = jnp.concatenate([total[0:24], total[24:48]], axis=1)
-    z_copies = [far_copy] + sum(far_copies + near_copies, [])
-    for copy in a_copies + g_copies + x_copies + z_copies:
+    z_copies = [far_copy] + sum(far_copies + near_copies + x_copies, [])
+    for copy in a_copies + g_copies + z_copies:
         copy.wait_send()
 
 
@@ -310,6 +330,7 @@
             pltpu.VMEM((QUADS, NX * NY * 4 * PAD, tokens), BF16),
             pltpu.VMEM((steps, NX * NY, 4 * PAD, HALF), BF16),
             pltpu.VMEM((steps, n_xy, 4 * PAD, HALF), BF16),
+            pltpu.VMEM((QUADS, 4 * PAD, HALF), BF16),
             pltpu.VMEM((4 * PAD, HALF), F32),
             pltpu.VMEM((QUADS, 4, 48, HALF), F32),
             pltpu.VMEM((QUADS, 4, 48, HALF), BF16),
@@ -332,6 +353,7 @@
             dma,
             dma((NZ - 1,)),
             dma((NZ - 1,)),
+            pltpu.SemaphoreType.REGULAR((2,)),
         ],
         compiler_params=pltpu.CompilerParams(
             collective_id=0, has_side_effects=True, vmem_limit_bytes=40 << 20

time: 50.1 us -> 49.7 us (level)
  no operation moved by 1% of the time
where the time goes in v3:
time: 49.7 us; the launch traced here: 49.6 us
  Pallas kernels  48.9 us (98%)
  between operations  0.64 us (1%)
    pallas_call x1, Pallas kernels, on_device(): pl.pallas_call(reduce_kernel, out_shape=(jax.ShapeDtypeStruct((24, rank),...  47.4 us
    pallas_call x1, Pallas kernels, on_device(): pl.pallas_call(step_kernel, out_shape=(jax.ShapeDtypeStruct((OWN, 1, rank...  1.52 us

profile of v3, /device:TPU:1, one launch (start us, length us, event | category | flops | bytes accessed | tf_op | source)
XLA Modules:
  0.0 49.6 jit_solution(13423378076357884632)
XLA Ops:
  0.6 47.4 %reduce_gradient.1 = (f32[24,256]{1,0:T(8,128)S(1)}, bf16[256,8192]{1,0:T(8,128)(2,1)S(1)}, f32[24,256]{1,0:T(8,128)S(1)}, f32[24,256]{1,0:T(8,128)S(1)}) custom-call(bf16[384,1024]{1,0:T(8,128)(2,1)} %act_hbm.1, bf16[8192,256]{1,0:T(8,128)(2,1)} %basis_hbm.1, bf16[1824,384]{1,0:T(8,128)(2,1)} %bitcast.6, f32[19,1,256]{2,1,0:T(1,128)} %bitcast.7, ...), custom_call_target="tpu_custom_call" | custom-call | tf_op jit(solution)/shard_map/reduce_gradient/pallas_call | solution.py:310
  48.1 1.5 %adam_update.1 = (f32[19,1,256]{2,1,0:T(1,128)}, f32[19,1,256]{2,1,0:T(1,128)}, bf16[19,8192]{1,0:T(8,128)(2,1)}) custom-call(f32[24,256]{1,0:T(8,128)S(1)} %get-tuple-element.10.grad, bf16[256,8192]{1,0:T(8,128)(2,1)S(1)} %get-tuple-element.11.turned, f32[24,256]{1,0:T(8,128)S(1)} %get-tuple-element.12.m, f32[24,256]{1,0:T(8,128)S(1)} %get-tuple-element.13.v), custom_call_target="tpu_custom_call" | custom-call | tf_op jit(solution)/shard_map/adam_update/pallas_call | solution.py:372

commit v4 on v3

--- a/solution.py
+++ b/solution.py
@@ -21,11 +21,11 @@
 HALF = 128
 
 TENSOR_PEERS = ((2, 0), (2, 1), (1, 0), (3, 0), (1, 1), (3, 1), (0, 1))
-XY_PEERS = ((2, 0), (1, 1), (3, 1), (1, 0), (3, 0), (0, 1))
-FAR_PEER = (2, 1)
-MERGED_ROUTES = (((1, 0), (1, 1)), ((3, 0), (3, 1)), ((2, 0), (2, 0)), ((1, 0), (1, 0)), ((3, 0), (3, 0)))
-DIRECT_ROUTES = tuple((p, p) for p in XY_PEERS)
-QUAD_STEPS = (1, 2, 0)
+XY_PEERS = ((2, 1), (2, 0), (1, 1), (3, 1), (1, 0), (3, 0), (0, 1))
+FIRST_ROUTES = (((1, 0), (1, 1)), ((3, 0), (3, 1)), ((1, 0), (1, 0)), ((3, 0), (3, 0)))
+SECOND_ROUTES = tuple((p, p) for p in XY_PEERS)
+MERGED = len(FIRST_ROUTES)
+GROUPS = ((6, 5, 7, 4), (8, 3, 9, 2), (10, 1, 11, 0))
 
 
 def reduce_kernel(
@@ -38,7 +38,6 @@
     dp, t = lax.axis_index("dp"), lax.axis_index("tensor")
     x, z, y = dp // (NZ * NY), lax.rem(dp // NY, NZ), lax.rem(dp, NY)
     yh, core = t // NC, lax.rem(t, NC)
-    own_quad, own_place = z // 4, lax.rem(z, 4)
     n_ten, n_xy = len(TENSOR_PEERS), len(XY_PEERS)
 
     def tensor_at(k):
@@ -61,8 +60,6 @@
         signal(dp, tensor_at(k))
     for dz in (3, 9, 2, 10, 1, 11):
         signal(dp_at(x, z + dz, y), t)
-    far_dp = dp_at(x + FAR_PEER[0], z, y + FAR_PEER[1])
-    signal(far_dp, t)
     for dx, dy in XY_PEERS:
         signal(dp_at(x + dx, z, y + dy), t)
 
@@ -101,7 +98,7 @@
         coded = jnp.dot(act[...], rows[:, h * HALF : (h + 1) * HALF], preferred_element_type=F32)
         part[h] = coded.astype(BF16).reshape(part.shape[1:])
         if h == 0:
-            pl.semaphore_wait(barrier, n_ten + 6 + 1 + n_xy)
+            pl.semaphore_wait(barrier, n_ten + 6 + n_xy)
             for i, dz in enumerate((3, NZ - 3)):
                 pl.semaphore_signal(
                     hello.at[i], inc=1, device_id=(dp_at(x, z + dz, y), t), device_id_type=MESH
@@ -117,19 +114,28 @@
             a_copies.append(copy)
 
     og_load.wait()
-    n_out, n_in = 16 * PAD, 16 * OWN
-    unit_rows = 8 * PAD
-    r = lax.broadcasted_iota(jnp.int32, (n_out, n_in), 0)
-    c = lax.broadcasted_iota(jnp.int32, (n_out, n_in), 1)
-    unit, in_unit = r // unit_rows, lax.rem(r, unit_rows)
-    place, line = in_unit // PAD, lax.rem(in_unit, PAD)
-    owner = unit * 8 + lax.rem(place, 4) * 2 + place // 4
-    pick = jnp.where((line < OWN) & (c == owner * OWN + line), 1.0, 0.0).astype(BF16)
-    for b in range(NX * NZ * NY // 16):
-        moved = jnp.dot(pick, og[b * n_in : (b + 1) * n_in, :], preferred_element_type=F32).astype(BF16)
-        for i in range(2):
-            ox, oq = (2 * b + i) // QUADS, (2 * b + i) % QUADS
-            ogp[oq, ox * unit_rows : (ox + 1) * unit_rows, :] = moved[i * unit_rows : (i + 1) * unit_rows, :]
+    unit_rows = NY * 4 * PAD
+    n_out, n_in = QUADS * unit_rows, NZ * NY * OWN
+    window = n_in + 8
+    r = lax.broadcasted_iota(jnp.int32, (n_out, 1), 0)
+    place, line = r // PAD, lax.rem(r, PAD)
+    group, in_group = place // (NY * 4), lax.rem(place, NY * 4)
+    ahead = jnp.zeros_like(r)
+    for a in range(QUADS):
+        for b in range(4):
+            ahead = jnp.where((group == a) & (lax.rem(in_group, 4) == b), GROUPS[a][b], ahead)
+    to_z = z + ahead
+    to_z = jnp.where(to_z >= NZ, to_z - NZ, to_z)
+    source = (to_z * NY + in_group // 4) * OWN + line
+    source = jnp.where(line < OWN, source, -window)
+    c = lax.broadcasted_iota(jnp.int32, (n_out, window), 1)
+    picks = [jnp.where(c == source + shift, 1.0, 0.0).astype(BF16) for shift in (0, 8)]
+    for ox in range(NX):
+        shift = ox * n_in % 16
+        first = ox * n_in - shift
+        moved = jnp.dot(picks[shift // 8], og[first : first + window, :], preferred_element_type=F32).astype(BF16)
+        for j in range(QUADS):
+            ogp[j, ox * unit_rows : (ox + 1) * unit_rows, :] = moved[j * unit_rows : (j + 1) * unit_rows, :]
     far_acc[...] = jnp.zeros_like(far_acc)
     near_acc[...] = jnp.zeros_like(near_acc)
 
@@ -163,60 +169,41 @@
 
     def along_z(src, dst, send_sem, recv_sem):
         copies = []
-        for j, ahead in enumerate(QUAD_STEPS):
+        for j, group in enumerate(GROUPS):
             copies.append([])
-            for e in range(0 if ahead else 1, 4):
-                zz = e if ahead else lax.rem(own_place + e, 4)
-                to = 4 * lax.rem(own_quad + ahead, QUADS) + zz
-                slot = lax.rem(to - z + NZ, NZ) - 1
-                copies[j].append(
-                    pltpu.make_async_remote_copy(
-                        src_ref=src.at[j, zz], dst_ref=dst.at[slot],
-                        send_sem=send_sem.at[4 * j + e - (not ahead)], recv_sem=recv_sem.at[slot],
-                        device_id=((x * NZ + to) * NY + y, t), device_id_type=MESH,
+            for zz, ahead in enumerate(group):
+                if ahead:
+                    copies[j].append(
+                        pltpu.make_async_remote_copy(
+                            src_ref=src.at[j, zz], dst_ref=dst.at[ahead - 1],
+                            send_sem=send_sem.at[ahead - 1], recv_sem=recv_sem.at[ahead - 1],
+                            device_id=(dp_at(x, z + ahead, y), t), device_id_type=MESH,
+                        )
                     )
-                )
         return copies
 
-    def sum_along_z(src, dst, recv_sem):
-        total = src[QUADS - 1, own_place].astype(F32)
-        for i in range(NZ - 1):
-            pltpu.make_async_copy(dst.at[i], dst.at[i], recv_sem.at[i]).wait()
-            total = total + dst[i].astype(F32)
+    def sum_along_z(src, copies):
+        total = src[QUADS - 1, 3].astype(F32)
+        for group, sent in zip(GROUPS, copies):
+            for ahead, copy in zip(group, sent):
+                copy.wait_recv()
+                total = total + copy.dst_ref[...].astype(F32)
         return total
 
     far_copies = along_z(far_send, far_in, f_send, f_recv)
     near_copies = along_z(near_send, near_in, z_send, z_recv)
-    far_place = lax.rem(x + FAR_PEER[0], NX) * NY + lax.rem(y + FAR_PEER[1], NY)
-    far_rows = pl.ds(pl.multiple_of(far_place * 4 * PAD, 4 * PAD), 4 * PAD)
+    two_x = lax.rem(x + 2, NX)
+    far_rows = pl.ds(pl.multiple_of(two_x * unit_rows, unit_rows), unit_rows)
     x_copies = [[] for _ in range(2 * QUADS)]
     for h in range(2):
         for k in range(n_ten):
             g_copies[h * n_ten + k].wait_recv()
         coded = code[h].reshape((n_ten + 1) * TOK, HALF)
-
-        def far_part():
-            for j, ahead in enumerate(QUAD_STEPS):
-                q = lax.rem(own_quad + ahead, QUADS)
-                acc[...] = jnp.dot(ogp[q, far_rows, :], coded, preferred_element_type=F32)
-                for zz in range(4):
-                    far_acc[j, zz, 24 * h : 24 * h + PAD, :] = acc[zz * PAD : (zz + 1) * PAD, :]
-
-        if h == 1:
-            far_part()
-            for i in range(2):
-                pl.semaphore_wait(hello.at[i], 1)
-            for j in range(QUADS):
-                for zz in range(4):
-                    far_send[j, zz] = far_acc[j, zz].astype(BF16)
-                for copy in far_copies[j]:
-                    copy.start()
-        for j, ahead in enumerate(QUAD_STEPS):
-            q = lax.rem(own_quad + ahead, QUADS)
+        for j in range(QUADS):
             at = h * QUADS + j
-            term = jnp.dot(ogp[q], coded, preferred_element_type=F32)
+            term = jnp.dot(ogp[j], coded, preferred_element_type=F32)
             chunk[at] = term.astype(BF16).reshape(chunk.shape[1:])
-            for k, (to, share) in enumerate(DIRECT_ROUTES if h else MERGED_ROUTES):
+            for k, (to, share) in enumerate(SECOND_ROUTES if h else FIRST_ROUTES):
                 px, py = xy_at(to)
                 sx, sy = xy_at(share)
                 copy = pltpu.make_async_remote_copy(
@@ -227,11 +214,18 @@
                 copy.start()
                 x_copies[at].append(copy)
         if h == 0:
-            far_part()
-
-    far_copy = pltpu.make_async_remote_copy(
-        src_ref=far_sum, dst_ref=far_got, send_sem=l_send, recv_sem=l_recv, device_id=(far_dp, t), device_id_type=MESH
-    )
+            for i in range(2):
+                pl.semaphore_wait(hello.at[i], 1)
+            for j in range(QUADS):
+                acc[...] = jnp.dot(ogp[j, far_rows, :], coded, preferred_element_type=F32)
+                for zz in range(4):
+                    for py in range(NY):
+                        at = (py * 4 + zz) * PAD
+                        far_acc[j, zz, 24 * py : 24 * py + PAD, :] = acc[at : at + PAD, :]
+                    far_send[j, zz] = far_acc[j, zz].astype(BF16)
+                for copy in far_copies[j]:
+                    copy.start()
+
     for j in range(QUADS):
         total = chunk[j, x * NY + 1 - y].astype(F32)
         for k in range(2):
@@ -239,22 +233,32 @@
             total = total + chunk_in[j, k].astype(F32)
         merged[j] = total.astype(BF16)
         copy = pltpu.make_async_remote_copy(
-            src_ref=merged.at[j], dst_ref=chunk_in.at[j, 5], send_sem=x_send.at[j, 5], recv_sem=x_recv.at[j, 5],
+            src_ref=merged.at[j], dst_ref=chunk_in.at[j, MERGED],
+            send_sem=x_send.at[j, MERGED], recv_sem=x_recv.at[j, MERGED],
             device_id=(dp_at(x, z, y + 1), t), device_id_type=MESH,
         )
         copy.start()
         x_copies[j].append(copy)
+    two_copies = []
     for j in range(QUADS):
         if j == QUADS - 1:
-            far_sum[...] = sum_along_z(far_send, far_in, f_recv).astype(BF16)
-            far_copy.start()
+            total = sum_along_z(far_send, far_copies)
+            blank = jnp.zeros((8, HALF), F32)
+            for py in range(NY):
+                far_sum[py] = jnp.concatenate([total[24 * py : 24 * py + 24], blank], axis=0).astype(BF16)
+                copy = pltpu.make_async_remote_copy(
+                    src_ref=far_sum.at[py], dst_ref=far_got.at[y], send_sem=l_send.at[py], recv_sem=l_recv.at[y],
+                    device_id=(dp_at(x + 2, z, py), t), device_id_type=MESH,
+                )
+                copy.start()
+                two_copies.append(copy)
         for h in range(2):
             at = h * QUADS + j
             total = chunk[at, x * NY + y].astype(F32)
-            for k in range(0 if h else 2, n_xy):
+            for k in range(0 if h else 2, len(x_copies[at])):
                 x_copies[at][k].wait_recv()
                 total = total + chunk_in[at, k].astype(F32)
-            acc[...] = total
+            acc[0 : 4 * PAD, :] = total
             for zz in range(4):
                 near_acc[j, zz, 24 * h : 24 * h + PAD, :] = acc[zz * PAD : (zz + 1) * PAD, :]
         for zz in range(4):
@@ -262,11 +266,13 @@
         for copy in near_copies[j]:
             copy.start()
 
-    total = sum_along_z(near_send, near_in, z_recv)
-    far_copy.wait_recv()
-    total = total + far_got[...].astype(F32)
-    grad_out[...] = jnp.concatenate([total[0:24], total[24:48]], axis=1)
-    z_copies = [far_copy] + sum(far_copies + near_copies + x_copies, [])
+    first = jnp.zeros((24, HALF), F32)
+    for py in range(NY):
+        pltpu.make_async_copy(far_got.at[py], far_got.at[py], l_recv.at[py]).wait()
+        first = first + far_got[py].astype(F32)[0:24]
+    total = sum_along_z(near_send, near_copies)
+    grad_out[...] = jnp.concatenate([total[0:24] + first, total[24:48]], axis=1)
+    z_copies = two_copies + sum(far_copies + near_copies + x_copies, [])
     for copy in a_copies + g_copies + z_copies:
         copy.wait_send()
 
@@ -331,12 +337,12 @@
             pltpu.VMEM((steps, NX * NY, 4 * PAD, HALF), BF16),
             pltpu.VMEM((steps, n_xy, 4 * PAD, HALF), BF16),
             pltpu.VMEM((QUADS, 4 * PAD, HALF), BF16),
-            pltpu.VMEM((4 * PAD, HALF), F32),
+            pltpu.VMEM((NY * 4 * PAD, HALF), F32),
             pltpu.VMEM((QUADS, 4, 48, HALF), F32),
             pltpu.VMEM((QUADS, 4, 48, HALF), BF16),
             pltpu.VMEM((NZ - 1, 48, HALF), BF16),
-            pltpu.VMEM((48, HALF), BF16),
-            pltpu.VMEM((48, HALF), BF16),
+            pltpu.VMEM((NY, 32, HALF), BF16),
+            pltpu.VMEM((NY, 32, HALF), BF16),
             pltpu.VMEM((QUADS, 4, 48, HALF), F32),
             pltpu.VMEM((QUADS, 4, 48, HALF), BF16),
             pltpu.VMEM((NZ - 1, 48, HALF), BF16),
@@ -349,8 +355,8 @@
             dma((steps, n_xy)),
             dma((NZ - 1,)),
             dma((NZ - 1,)),
-            dma,
-            dma,
+            dma((NY,)),
+            dma((NY,)),
             dma((NZ - 1,)),
             dma((NZ - 1,)),
             pltpu.SemaphoreType.REGULAR((2,)),

time: 49.7 us -> 51.3 us (1.032)
  Pallas kernels: 48.9 us -> 50.5 us
    pallas_call x1, Pallas kernels: 47.4 us -> 49 us  [on_device(): pl.pallas_call(reduce_kernel, out_shape=(jax.ShapeDtypeStruct((24, rank),...]
where the time goes in v4:
time: 51.3 us; the launch traced here: 51.1 us
  Pallas kernels  50.5 us (98%)
  between operations  0.64 us (1%)
    pallas_call x1, Pallas kernels, on_device(): pl.pallas_call(reduce_kernel, out_shape=(jax.ShapeDtypeStruct((24, rank),...  49 us
    pallas_call x1, Pallas kernels, on_device(): pl.pallas_call(step_kernel, out_shape=(jax.ShapeDtypeStruct((OWN, 1, rank...  1.52 us

profile of v4, /device:TPU:1, one launch (start us, length us, event | category | flops | bytes accessed | tf_op | source)
XLA Modules:
  0.0 51.1 jit_solution(5109174440027783840)
XLA Ops:
  0.6 49.0 %reduce_gradient.1 = (f32[24,256]{1,0:T(8,128)S(1)}, bf16[256,8192]{1,0:T(8,128)(2,1)S(1)}, f32[24,256]{1,0:T(8,128)S(1)}, f32[24,256]{1,0:T(8,128)S(1)}) custom-call(bf16[384,1024]{1,0:T(8,128)(2,1)} %act_hbm.1, bf16[8192,256]{1,0:T(8,128)(2,1)} %basis_hbm.1, bf16[1824,384]{1,0:T(8,128)(2,1)} %bitcast.6, f32[19,1,256]{2,1,0:T(1,128)} %bitcast.7, ...), custom_call_target="tpu_custom_call" | custom-call | tf_op jit(solution)/shard_map/reduce_gradient/pallas_call | solution.py:316
  49.6 1.5 %adam_update.1 = (f32[19,1,256]{2,1,0:T(1,128)}, f32[19,1,256]{2,1,0:T(1,128)}, bf16[19,8192]{1,0:T(8,128)(2,1)}) custom-call(f32[24,256]{1,0:T(8,128)S(1)} %get-tuple-element.10.grad, bf16[256,8192]{1,0:T(8,128)(2,1)S(1)} %get-tuple-element.11.turned, f32[24,256]{1,0:T(8,128)S(1)} %get-tuple-element.12.m, f32[24,256]{1,0:T(8,128)S(1)} %get-tuple-element.13.v), custom_call_target="tpu_custom_call" | custom-call | tf_op jit(solution)/shard_map/adam_update/pallas_call | solution.py:378

commit v5 on v2

--- a/solution.py
+++ b/solution.py
@@ -21,30 +21,27 @@
 HALF = 128
 
 TENSOR_PEERS = ((2, 0), (2, 1), (1, 0), (3, 0), (1, 1), (3, 1), (0, 1))
-XY_PEERS = ((2, 0), (1, 1), (3, 1), (1, 0), (3, 0), (0, 1))
-FAR_PEER = (2, 1)
-QUAD_STEPS = (1, 2, 0)
+XY_PEERS = ((2, 1), (2, 0), (1, 1), (3, 1), (1, 0), (3, 0), (0, 1))
 
 
 def reduce_kernel(
     act_hbm, basis_hbm, og_hbm, m_hbm, v_hbm,
     grad_out, turned_out, m_out, v_out,
     act, rows, basis, og, m_in, v_in,
-    part, part_in, code, ogp, chunk, chunk_in, acc, far_acc, far_send, far_in, far_sum, far_got, near_acc, near_send, near_in,
-    load_sem, a_send, a_recv, g_send, g_recv, x_send, x_recv, f_send, f_recv, l_send, l_recv, z_send, z_recv,
+    part, part_in, code, ogp, chunk, chunk_in, acc, cut, z_out, z_in,
+    load_sem, a_send, a_recv, g_send, g_recv, x_send, x_recv, z_send, z_recv, hello,
 ):
     dp, t = lax.axis_index("dp"), lax.axis_index("tensor")
     x, z, y = dp // (NZ * NY), lax.rem(dp // NY, NZ), lax.rem(dp, NY)
     yh, core = t // NC, lax.rem(t, NC)
-    own_quad, own_place = z // 4, lax.rem(z, 4)
     n_ten, n_xy = len(TENSOR_PEERS), len(XY_PEERS)
 
     def tensor_at(k):
         a, c = TENSOR_PEERS[k]
         return lax.rem(yh + a, NYH) * NC + lax.rem(core + c, NC)
 
-    def xy_at(k):
-        dx, dy = XY_PEERS[k]
+    def xy_at(place):
+        dx, dy = place
         return lax.rem(x + dx, NX), lax.rem(y + dy, NY)
 
     def dp_at(px, pz, py):
@@ -55,14 +52,15 @@
     def signal(to_dp, to_t):
         pl.semaphore_signal(barrier, inc=1, device_id=(to_dp, to_t), device_id_type=MESH)
 
-    for dz in (6, 5, 7, 4, 8, 3, 9, 2, 10, 1, 11):
-        signal(dp_at(x, z + dz, y), t)
     for k in range(n_ten):
         signal(dp, tensor_at(k))
-    far_dp = dp_at(x + FAR_PEER[0], z, y + FAR_PEER[1])
-    signal(far_dp, t)
     for dx, dy in XY_PEERS:
         signal(dp_at(x + dx, z, y + dy), t)
+    for to in range(NZ - 1, 0, -1):
+
+        @pl.when(z < to)
+        def _():
+            signal(dp_at(x, to, y), t)
 
     tokens, feats = act.shape
     start = pl.multiple_of(t * feats, feats)
@@ -99,7 +97,7 @@
         coded = jnp.dot(act[...], rows[:, h * HALF : (h + 1) * HALF], preferred_element_type=F32)
         part[h] = coded.astype(BF16).reshape(part.shape[1:])
         if h == 0:
-            pl.semaphore_wait(barrier, NZ - 1 + n_ten + 1 + n_xy)
+            pl.semaphore_wait(barrier, n_ten + n_xy + z)
         for k in range(n_ten):
             peer = tensor_at(k)
             copy = pltpu.make_async_remote_copy(
@@ -109,6 +107,12 @@
             )
             copy.start()
             a_copies.append(copy)
+
+    for to in range(NZ - 1):
+
+        @pl.when(z > to)
+        def _():
+            pl.semaphore_signal(hello.at[z], inc=1, device_id=(dp_at(x, to, y), t), device_id_type=MESH)
 
     og_load.wait()
     n_out, n_in = 16 * PAD, 16 * OWN
@@ -124,8 +128,7 @@
         for i in range(2):
             ox, oq = (2 * b + i) // QUADS, (2 * b + i) % QUADS
             ogp[oq, ox * unit_rows : (ox + 1) * unit_rows, :] = moved[i * unit_rows : (i + 1) * unit_rows, :]
-    far_acc[...] = jnp.zeros_like(far_acc)
-    near_acc[...] = jnp.zeros_like(near_acc)
+    cut[...] = jnp.zeros_like(cut)
 
     g_copies = []
     for h in range(2):
@@ -155,99 +158,77 @@
     for i in range(basis.shape[0] // wide):
         turned_out[:, i * wide : (i + 1) * wide] = basis[i * wide : (i + 1) * wide, :].T
 
-    def along_z(src, dst, send_sem, recv_sem):
-        copies = []
-        for j, ahead in enumerate(QUAD_STEPS):
-            copies.append([])
-            for e in range(0 if ahead else 1, 4):
-                zz = e if ahead else lax.rem(own_place + e, 4)
-                to = 4 * lax.rem(own_quad + ahead, QUADS) + zz
-                slot = lax.rem(to - z + NZ, NZ) - 1
-                copies[j].append(
-                    pltpu.make_async_remote_copy(
-                        src_ref=src.at[j, zz], dst_ref=dst.at[slot],
-                        send_sem=send_sem.at[4 * j + e - (not ahead)], recv_sem=recv_sem.at[slot],
-                        device_id=((x * NZ + to) * NY + y, t), device_id_type=MESH,
-                    )
-                )
-        return copies
-
-    def sum_along_z(src, dst, recv_sem):
-        total = src[QUADS - 1, own_place].astype(F32)
-        for i in range(NZ - 1):
-            pltpu.make_async_copy(dst.at[i], dst.at[i], recv_sem.at[i]).wait()
-            total = total + dst[i].astype(F32)
-        return total
-
-    far_copies = along_z(far_send, far_in, f_send, f_recv)
-    near_copies = along_z(near_send, near_in, z_send, z_recv)
-    far_place = lax.rem(x + FAR_PEER[0], NX) * NY + lax.rem(y + FAR_PEER[1], NY)
-    far_rows = pl.ds(pl.multiple_of(far_place * 4 * PAD, 4 * PAD), 4 * PAD)
-    x_copies = []
+    def z_copy(to):
+        return pltpu.make_async_remote_copy(
+            src_ref=z_out.at[to], dst_ref=z_in.at[z], send_sem=z_send.at[to], recv_sem=z_recv.at[z],
+            device_id=(dp_at(x, to, y), t), device_id_type=MESH,
+        )
+
+    x_copies = {}
+
+    def share(h, q):
+        coded = code[h].reshape((n_ten + 1) * TOK, HALF)
+        at = h * QUADS + q
+        term = jnp.dot(ogp[q], coded, preferred_element_type=F32)
+        chunk[at] = term.astype(BF16).reshape(chunk.shape[1:])
+        x_copies[at] = []
+        for k in range(n_xy):
+            px, py = xy_at(XY_PEERS[k])
+            copy = pltpu.make_async_remote_copy(
+                src_ref=chunk.at[at, px * NY + py], dst_ref=chunk_in.at[at, k],
+                send_sem=x_send.at[at, k], recv_sem=x_recv.at[at, k],
+                device_id=((px * NZ + z) * NY + py, t), device_id_type=MESH,
+            )
+            copy.start()
+            x_copies[at].append(copy)
+
+    def collect(q):
+        for h in range(2):
+            at = h * QUADS + q
+            total = chunk[at, x * NY + y].astype(F32)
+            for k in range(n_xy):
+                x_copies[at][k].wait_recv()
+                total = total + chunk_in[at, k].astype(F32)
+            acc[...] = total
+            for zz in range(4):
+                cut[zz, 24 * h : 24 * h + PAD, :] = acc[zz * PAD : (zz + 1) * PAD, :]
+        for zz in range(4):
+            to = 4 * q + zz
+            z_out[to] = cut[zz].astype(BF16)
+
+            @pl.when(z < to)
+            def _():
+                pl.semaphore_wait(hello.at[to], 1)
+
+            @pl.when(z != to)
+            def _():
+                z_copy(to).start()
+
     for h in range(2):
         for k in range(n_ten):
             g_copies[h * n_ten + k].wait_recv()
-        coded = code[h].reshape((n_ten + 1) * TOK, HALF)
-
-        def far_part():
-            for j, ahead in enumerate(QUAD_STEPS):
-                q = lax.rem(own_quad + ahead, QUADS)
-                acc[...] = jnp.dot(ogp[q, far_rows, :], coded, preferred_element_type=F32)
-                for zz in range(4):
-                    far_acc[j, zz, 24 * h : 24 * h + PAD, :] = acc[zz * PAD : (zz + 1) * PAD, :]
-
-        if h == 1:
-            far_part()
-            for j in range(QUADS):
-                for zz in range(4):
-                    far_send[j, zz] = far_acc[j, zz].astype(BF16)
-                for copy in far_copies[j]:
-                    copy.start()
-        for j, ahead in enumerate(QUAD_STEPS):
-            q = lax.rem(own_quad + ahead, QUADS)
-            at = h * QUADS + j
-            term = jnp.dot(ogp[q], coded, preferred_element_type=F32)
-            chunk[at] = term.astype(BF16).reshape(chunk.shape[1:])
-            for k in range(n_xy):
-                px, py = xy_at(k)
-                copy = pltpu.make_async_remote_copy(
-                    src_ref=chunk.at[at, px * NY + py], dst_ref=chunk_in.at[at, k],
-                    send_sem=x_send.at[at, k], recv_sem=x_recv.at[at, k],
-                    device_id=((px * NZ + z) * NY + py, t), device_id_type=MESH,
-                )
-                copy.start()
-                x_copies.append(copy)
-        if h == 0:
-            far_part()
-
-    far_copy = pltpu.make_async_remote_copy(
-        src_ref=far_sum, dst_ref=far_got, send_sem=l_send, recv_sem=l_recv, device_id=(far_dp, t), device_id_type=MESH
-    )
-    for h in range(2):
-        for j in range(QUADS):
-            at = h * QUADS + j
-            if at == 2 * QUADS - 1:
-                far_sum[...] = sum_along_z(far_send, far_in, f_recv).astype(BF16)
-                far_copy.start()
-            total = chunk[at, x * NY + y].astype(F32)
-            for k in range(n_xy):
-                x_copies[at * n_xy + k].wait_recv()
-                total = total + chunk_in[at, k].astype(F32)
-            acc[...] = total
-            for zz in range(4):
-                near_acc[j, zz, 24 * h : 24 * h + PAD, :] = acc[zz * PAD : (zz + 1) * PAD, :]
-            if h == 1:
-                for zz in range(4):
-                    near_send[j, zz] = near_acc[j, zz].astype(BF16)
-                for copy in near_copies[j]:
-                    copy.start()
-
-    total = sum_along_z(near_send, near_in, z_recv)
-    far_copy.wait_recv()
-    total = total + far_got[...].astype(F32)
+        share(h, 0)
+    share(0, 1)
+    for q in range(QUADS):
+        collect(q)
+        if q + 1 < QUADS:
+            share(1, q + 1)
+        if q + 2 < QUADS:
+            share(0, q + 2)
+
+    total = z_out[z].astype(F32)
+    for ahead in range(1, NZ):
+        sender = lax.rem(z + ahead, NZ)
+        pltpu.make_async_copy(z_in.at[sender], z_in.at[sender], z_recv.at[sender]).wait()
+        total = total + z_in[sender].astype(F32)
     grad_out[...] = jnp.concatenate([total[0:24], total[24:48]], axis=1)
-    z_copies = [far_copy] + sum(far_copies + near_copies, [])
-    for copy in a_copies + g_copies + x_copies + z_copies:
+    for to in range(NZ):
+
+        @pl.when(z != to)
+        def _():
+            z_copy(to).wait_send()
+
+    for copy in a_copies + g_copies + sum(x_copies.values(), []):
         copy.wait_send()
 
 
@@ -311,14 +292,9 @@
             pltpu.VMEM((steps, NX * NY, 4 * PAD, HALF), BF16),
             pltpu.VMEM((steps, n_xy, 4 * PAD, HALF), BF16),
             pltpu.VMEM((4 * PAD, HALF), F32),
-            pltpu.VMEM((QUADS, 4, 48, HALF), F32),
-            pltpu.VMEM((QUADS, 4, 48, HALF), BF16),
-            pltpu.VMEM((NZ - 1, 48, HALF), BF16),
-            pltpu.VMEM((48, HALF), BF16),
-            pltpu.VMEM((48, HALF), BF16),
-            pltpu.VMEM((QUADS, 4, 48, HALF), F32),
-            pltpu.VMEM((QUADS, 4, 48, HALF), BF16),
-            pltpu.VMEM((NZ - 1, 48, HALF), BF16),
+            pltpu.VMEM((4, 48, HALF), F32),
+            pltpu.VMEM((NZ, 48, HALF), BF16),
+            pltpu.VMEM((NZ, 48, HALF), BF16),
             dma((12,)),
             dma((2, n_ten)),
             dma((2, n_ten)),
@@ -326,12 +302,9 @@
             dma((2, n_ten)),
             dma((steps, n_xy)),
             dma((steps, n_xy)),
-            dma((NZ - 1,)),
-            dma((NZ - 1,)),
-            dma,
-            dma,
-            dma((NZ - 1,)),
-            dma((NZ - 1,)),
+            dma((NZ,)),
+            dma((NZ,)),
+            pltpu.SemaphoreType.REGULAR((NZ,)),
         ],
         compiler_params=pltpu.CompilerParams(
             collective_id=0, has_side_effects=True, vmem_limit_bytes=40 << 20

time: 50.1 us -> 47.4 us (0.946); the launches traced: 49.5 us -> 47.3 us
  Pallas kernels: 48.8 us -> 46.6 us
    pallas_call x1, Pallas kernels: 47.3 us -> 45.1 us  [on_device(): pl.pallas_call(reduce_kernel, out_shape=(jax.ShapeDtypeStruct((24, rank),...]
where the time goes in v5:
time: 47.4 us; the launch traced here: 47.3 us
  Pallas kernels  46.6 us (98%)
  between operations  0.64 us (1%)
    pallas_call x1, Pallas kernels, on_device(): pl.pallas_call(reduce_kernel, out_shape=(jax.ShapeDtypeStruct((24, rank),...  45.1 us
    pallas_call x1, Pallas kernels, on_device(): pl.pallas_call(step_kernel, out_shape=(jax.ShapeDtypeStruct((OWN, 1, rank...  1.52 us

profile of v5, /device:TPU:1, one launch (start us, length us, event | category | flops | bytes accessed | tf_op | source)
XLA Modules:
  0.0 47.3 jit_solution(12613904629359269769)
XLA Ops:
  0.6 45.1 %reduce_gradient.1 = (f32[24,256]{1,0:T(8,128)S(1)}, bf16[256,8192]{1,0:T(8,128)(2,1)S(1)}, f32[24,256]{1,0:T(8,128)S(1)}, f32[24,256]{1,0:T(8,128)S(1)}) custom-call(bf16[384,1024]{1,0:T(8,128)(2,1)} %act_hbm.1, bf16[8192,256]{1,0:T(8,128)(2,1)} %basis_hbm.1, bf16[1824,384]{1,0:T(8,128)(2,1)} %bitcast.6, f32[19,1,256]{2,1,0:T(1,128)} %bitcast.7, ...), custom_call_target="tpu_custom_call" | custom-call | tf_op jit(solution)/shard_map/reduce_gradient/pallas_call | solution.py:271
  45.8 1.5 %adam_update.1 = (f32[19,1,256]{2,1,0:T(1,128)}, f32[19,1,256]{2,1,0:T(1,128)}, bf16[19,8192]{1,0:T(8,128)(2,1)}) custom-call(f32[24,256]{1,0:T(8,128)S(1)} %get-tuple-element.10.grad, bf16[256,8192]{1,0:T(8,128)(2,1)S(1)} %get-tuple-element.11.turned, f32[24,256]{1,0:T(8,128)S(1)} %get-tuple-element.12.m, f32[24,256]{1,0:T(8,128)S(1)} %get-tuple-element.13.v), custom_call_target="tpu_custom_call" | custom-call | tf_op jit(solution)/shard_map/adam_update/pallas_call | solution.py:323

commit v6 on v5

--- a/solution.py
+++ b/solution.py
@@ -16,7 +16,11 @@
 NYH, NC = 4, 2
 OWN = 19
 PAD = 20
-QUADS = NZ // 4
+SIZES = (1, 3, 4, 4)
+ROWS = (32, 64, 80, 80)
+STARTS = (0, 1, 4, 8)
+FIRST_ROW = (0, 32, 96, 176)
+ALL_ROWS = 256
 TOK = 48
 HALF = 128
 
@@ -115,19 +119,23 @@
             pl.semaphore_signal(hello.at[z], inc=1, device_id=(dp_at(x, to, y), t), device_id_type=MESH)
 
     og_load.wait()
-    n_out, n_in = 16 * PAD, 16 * OWN
-    unit_rows = 8 * PAD
-    r = lax.broadcasted_iota(jnp.int32, (n_out, n_in), 0)
-    c = lax.broadcasted_iota(jnp.int32, (n_out, n_in), 1)
-    unit, in_unit = r // unit_rows, lax.rem(r, unit_rows)
-    place, line = in_unit // PAD, lax.rem(in_unit, PAD)
-    owner = unit * 8 + lax.rem(place, 4) * 2 + place // 4
-    pick = jnp.where((line < OWN) & (c == owner * OWN + line), 1.0, 0.0).astype(BF16)
-    for b in range(NX * NZ * NY // 16):
-        moved = jnp.dot(pick, og[b * n_in : (b + 1) * n_in, :], preferred_element_type=F32).astype(BF16)
-        for i in range(2):
-            ox, oq = (2 * b + i) // QUADS, (2 * b + i) % QUADS
-            ogp[oq, ox * unit_rows : (ox + 1) * unit_rows, :] = moved[i * unit_rows : (i + 1) * unit_rows, :]
+    n_in = NZ * NY * OWN
+    window = n_in + 8
+    r = lax.broadcasted_iota(jnp.int32, (NY * ALL_ROWS, 1), 0)
+    to_y, row = r // ALL_ROWS, lax.rem(r, ALL_ROWS)
+    source = jnp.full_like(r, -window)
+    for g in range(len(SIZES)):
+        for i in range(SIZES[g]):
+            at = FIRST_ROW[g] + i * PAD
+            inside = (row >= at) & (row < at + OWN)
+            source = jnp.where(inside, ((STARTS[g] + i) * NY + to_y) * OWN + row - at, source)
+    c = lax.broadcasted_iota(jnp.int32, (NY * ALL_ROWS, window), 1)
+    picks = [jnp.where(c == source + shift, 1.0, 0.0).astype(BF16) for shift in (0, 8)]
+    for ox in range(NX):
+        shift = ox * n_in % 16
+        first = ox * n_in - shift
+        moved = jnp.dot(picks[shift // 8], og[first : first + window, :], preferred_element_type=F32)
+        ogp[ox * NY : (ox + 1) * NY] = moved.astype(BF16).reshape(NY, ALL_ROWS, moved.shape[1])
     cut[...] = jnp.zeros_like(cut)
 
     g_copies = []
@@ -166,35 +174,37 @@
 
     x_copies = {}
 
-    def share(h, q):
+    def share(h, g):
         coded = code[h].reshape((n_ten + 1) * TOK, HALF)
-        at = h * QUADS + q
-        term = jnp.dot(ogp[q], coded, preferred_element_type=F32)
-        chunk[at] = term.astype(BF16).reshape(chunk.shape[1:])
+        at, n = h * len(SIZES) + g, ROWS[g]
+        rows_of = ogp[:, FIRST_ROW[g] : FIRST_ROW[g] + n, :].reshape(NX * NY * n, ogp.shape[2])
+        term = jnp.dot(rows_of, coded, preferred_element_type=F32)
+        chunk[at, :, 0:n, :] = term.astype(BF16).reshape(NX * NY, n, HALF)
         x_copies[at] = []
         for k in range(n_xy):
             px, py = xy_at(XY_PEERS[k])
             copy = pltpu.make_async_remote_copy(
-                src_ref=chunk.at[at, px * NY + py], dst_ref=chunk_in.at[at, k],
+                src_ref=chunk.at[at, px * NY + py, pl.ds(0, n)], dst_ref=chunk_in.at[at, k, pl.ds(0, n)],
                 send_sem=x_send.at[at, k], recv_sem=x_recv.at[at, k],
                 device_id=((px * NZ + z) * NY + py, t), device_id_type=MESH,
             )
             copy.start()
             x_copies[at].append(copy)
 
-    def collect(q):
+    def collect(g):
+        n = ROWS[g]
         for h in range(2):
-            at = h * QUADS + q
-            total = chunk[at, x * NY + y].astype(F32)
+            at = h * len(SIZES) + g
+            total = chunk[at, x * NY + y, 0:n, :].astype(F32)
             for k in range(n_xy):
                 x_copies[at][k].wait_recv()
-                total = total + chunk_in[at, k].astype(F32)
-            acc[...] = total
-            for zz in range(4):
-                cut[zz, 24 * h : 24 * h + PAD, :] = acc[zz * PAD : (zz + 1) * PAD, :]
-        for zz in range(4):
-            to = 4 * q + zz
-            z_out[to] = cut[zz].astype(BF16)
+                total = total + chunk_in[at, k, 0:n, :].astype(F32)
+            acc[0:n, :] = total
+            for i in range(SIZES[g]):
+                cut[i, 24 * h : 24 * h + PAD, :] = acc[i * PAD : (i + 1) * PAD, :]
+        for i in range(SIZES[g]):
+            to = STARTS[g] + i
+            z_out[to] = cut[i].astype(BF16)
 
             @pl.when(z < to)
             def _():
@@ -209,13 +219,12 @@
             g_copies[h * n_ten + k].wait_recv()
         share(h, 0)
     share(0, 1)
-    for q in range(QUADS):
-        collect(q)
-        if q + 1 < QUADS:
-            share(1, q + 1)
-        if q + 2 < QUADS:
-            share(0, q + 2)
-
+    for g in range(len(SIZES)):
+        collect(g)
+        if g + 1 < len(SIZES):
+            share(1, g + 1)
+        if g + 2 < len(SIZES):
+            share(0, g + 2)
     total = z_out[z].astype(F32)
     for ahead in range(1, NZ):
         sender = lax.rem(z + ahead, NZ)
@@ -267,7 +276,7 @@
     vmem = pl.BlockSpec(memory_space=pltpu.VMEM)
     dma = pltpu.SemaphoreType.DMA
     n_ten, n_xy = len(TENSOR_PEERS), len(XY_PEERS)
-    steps = 2 * QUADS
+    steps = 2 * len(SIZES)
     grad, turned, m, v = pl.pallas_call(
         reduce_kernel,
         out_shape=(
@@ -288,7 +297,7 @@
             pltpu.VMEM((2, n_ten + 1, TOK, HALF), BF16),
             pltpu.VMEM((2, n_ten, TOK, HALF), BF16),
             pltpu.VMEM((2, n_ten + 1, TOK, HALF), BF16),
-            pltpu.VMEM((QUADS, NX * NY * 4 * PAD, tokens), BF16),
+            pltpu.VMEM((NX * NY, ALL_ROWS, tokens), BF16),
             pltpu.VMEM((steps, NX * NY, 4 * PAD, HALF), BF16),
             pltpu.VMEM((steps, n_xy, 4 * PAD, HALF), BF16),
             pltpu.VMEM((4 * PAD, HALF), F32),

time: 47.4 us -> 49.2 us (1.038)
  the two profiles are of different devices: /device:TPU:1 before, /device:TPU:256 now
where the time goes in v6:
time: 49.2 us; the launch traced here: 49.1 us
  Pallas kernels  48.4 us (98%)
  between operations  0.64 us (1%)
    pallas_call x1, Pallas kernels, on_device(): pl.pallas_call(reduce_kernel, out_shape=(jax.ShapeDtypeStruct((24, rank),...  46.9 us
    pallas_call x1, Pallas kernels, on_device(): pl.pallas_call(step_kernel, out_shape=(jax.ShapeDtypeStruct((OWN, 1, rank...  1.52 us

profile of v6, /device:TPU:256, one launch (start us, length us, event | category | flops | bytes accessed | tf_op | source)
XLA Modules:
  0.0 49.1 jit_solution(6425809998408803389)
XLA Ops:
  0.6 46.9 %reduce_gradient.1 = (f32[24,256]{1,0:T(8,128)S(1)}, bf16[256,8192]{1,0:T(8,128)(2,1)S(1)}, f32[24,256]{1,0:T(8,128)S(1)}, f32[24,256]{1,0:T(8,128)S(1)}) custom-call(bf16[384,1024]{1,0:T(8,128)(2,1)} %act_hbm.1, bf16[8192,256]{1,0:T(8,128)(2,1)} %basis_hbm.1, bf16[1824,384]{1,0:T(8,128)(2,1)} %bitcast.6, f32[19,1,256]{2,1,0:T(1,128)} %bitcast.7, ...), custom_call_target="tpu_custom_call" | custom-call | tf_op jit(solution)/shard_map/reduce_gradient/pallas_call | solution.py:280
  47.6 1.5 %adam_update.1 = (f32[19,1,256]{2,1,0:T(1,128)}, f32[19,1,256]{2,1,0:T(1,128)}, bf16[19,8192]{1,0:T(8,128)(2,1)}) custom-call(f32[24,256]{1,0:T(8,128)S(1)} %get-tuple-element.10.grad, bf16[256,8192]{1,0:T(8,128)(2,1)S(1)} %get-tuple-element.11.turned, f32[24,256]{1,0:T(8,128)S(1)} %get-tuple-element.12.m, f32[24,256]{1,0:T(8,128)S(1)} %get-tuple-element.13.v), custom_call_target="tpu_custom_call" | custom-call | tf_op jit(solution)/shard_map/adam_update/pallas_call | solution.py:332

commit v7 on v6

--- a/solution.py
+++ b/solution.py
@@ -218,13 +218,11 @@
         for k in range(n_ten):
             g_copies[h * n_ten + k].wait_recv()
         share(h, 0)
-    share(0, 1)
     for g in range(len(SIZES)):
+        if g + 1 < len(SIZES):
+            for h in range(2):
+                share(h, g + 1)
         collect(g)
-        if g + 1 < len(SIZES):
-            share(1, g + 1)
-        if g + 2 < len(SIZES):
-            share(0, g + 2)
     total = z_out[z].astype(F32)
     for ahead in range(1, NZ):
         sender = lax.rem(z + ahead, NZ)

time: 49.2 us -> 46.6 us (0.947)
  Pallas kernels: 48.4 us -> 45.8 us
    pallas_call x1, Pallas kernels: 46.9 us -> 44.3 us  [on_device(): pl.pallas_call(reduce_kernel, out_shape=(jax.ShapeDtypeStruct((24, rank),...]
where the time goes in v7:
time: 46.6 us; the launch traced here: 46.5 us
  Pallas kernels  45.8 us (98%)
  between operations  0.64 us (1%)
    pallas_call x1, Pallas kernels, on_device(): pl.pallas_call(reduce_kernel, out_shape=(jax.ShapeDtypeStruct((24, rank),...  44.3 us
    pallas_call x1, Pallas kernels, on_device(): pl.pallas_call(step_kernel, out_shape=(jax.ShapeDtypeStruct((OWN, 1, rank...  1.52 us

profile of v7, /device:TPU:256, one launch (start us, length us, event | category | flops | bytes accessed | tf_op | source)
XLA Modules:
  0.0 46.5 jit_solution(13193651317094450475)
XLA Ops:
  0.6 44.3 %reduce_gradient.1 = (f32[24,256]{1,0:T(8,128)S(1)}, bf16[256,8192]{1,0:T(8,128)(2,1)S(1)}, f32[24,256]{1,0:T(8,128)S(1)}, f32[24,256]{1,0:T(8,128)S(1)}) custom-call(bf16[384,1024]{1,0:T(8,128)(2,1)} %act_hbm.1, bf16[8192,256]{1,0:T(8,128)(2,1)} %basis_hbm.1, bf16[1824,384]{1,0:T(8,128)(2,1)} %bitcast.6, f32[19,1,256]{2,1,0:T(1,128)} %bitcast.7, ...), custom_call_target="tpu_custom_call" | custom-call | tf_op jit(solution)/shard_map/reduce_gradient/pallas_call | solution.py:278
  44.9 1.5 %adam_update.1 = (f32[19,1,256]{2,1,0:T(1,128)}, f32[19,1,256]{2,1,0:T(1,128)}, bf16[19,8192]{1,0:T(8,128)(2,1)}) custom-call(f32[24,256]{1,0:T(8,128)S(1)} %get-tuple-element.10.grad, bf16[256,8192]{1,0:T(8,128)(2,1)S(1)} %get-tuple-element.11.turned, f32[24,256]{1,0:T(8,128)S(1)} %get-tuple-element.12.m, f32[24,256]{1,0:T(8,128)S(1)} %get-tuple-element.13.v), custom_call_target="tpu_custom_call" | custom-call | tf_op jit(solution)/shard_map/adam_update/pallas_call | solution.py:330
